TPU v7x, 256 devices: a whole 4x4x8 slice. The times are simulated.
256 devices in a mesh: dp: 16 (over z, core), seq: 16 (over x, y).
Axes of the slice: x: 4, y: 4, z: 8, core: 2. Of those that a mesh axis runs over, the one named last changes fastest.
Arguments:
- queries: bfloat16 [32768, 2048], P(('dp', 'seq')), may hold values from -10 to 10
- keys: bfloat16 [32768, 2048], P(('dp', 'seq')), may hold values from -10 to 10
- values: bfloat16 [32768, 2048], P(('dp', 'seq')), may hold values from -6 to 6
- attn: bfloat16 [32768, 2048], P(('dp', 'seq')), may hold values from -6 to 6
- grad_out: bfloat16 [32768, 4096], P(('dp', 'seq')), may hold values from -24 to 24
- w_out: bfloat16 [2048, 4096], P('seq'), may hold values from -0.125 to 0.125
- starts: int32 [16, 8], P('dp'), may hold values from 0 to 2047, as said below
Outputs:
- grad_queries: bfloat16 [32768, 2048], P(('dp', 'seq'))
- grad_keys: bfloat16 [32768, 2048], P(('dp', 'seq'))
- grad_values: bfloat16 [32768, 2048], P(('dp', 'seq'))
- grad_w_out: float32 [2048, 4096], P('seq', 'dp')
Inputs may be any that keep to these rules, and one draw needn't show every extreme that they name: starts[r, 0] = 0 and each row is strictly increasing.
All inputs are finite; a program needn't handle non-finite values.
Results may differ from a plain program's by a relative error of at most 0.022.
Values may be sent and summed in bfloat16 or wider, within the bound.
A program may use at most 128 MiB of HBM per device.

v0:
```python
import jax
import jax.numpy as jnp
from jax import lax
from jax.sharding import PartitionSpec as P

HDIM = 128


def tile_scores(q_blk, key_tile, pos_blk, seg_blk, key_pos, scale):
    scores = jnp.einsum("qhd,khd->hqk", q_blk, key_tile, preferred_element_type=jnp.float32) * scale
    live = (key_pos[None, :] <= pos_blk[:, None]) & (key_pos[None, :] >= seg_blk[:, None])
    return (scores, live[None])


def tile_grads(scores, live, top, total, q_blk, g_blk, row_dot, key_tile, val_tile):
    prob = jnp.where(live, jnp.exp(scores - top), 0.0) / total
    prob_b = prob.astype(jnp.bfloat16)
    grad_v = jnp.einsum("hqk,qhd->khd", prob_b, g_blk, preferred_element_type=jnp.float32)
    grad_prob = jnp.einsum("qhd,khd->hqk", g_blk, val_tile, preferred_element_type=jnp.float32)
    grad_s = (prob * (grad_prob - row_dot)).astype(jnp.bfloat16)
    grad_q = jnp.einsum("hqk,khd->qhd", grad_s, key_tile, preferred_element_type=jnp.float32)
    grad_k = jnp.einsum("hqk,qhd->khd", grad_s, q_blk, preferred_element_type=jnp.float32)
    return (grad_q, grad_k, grad_v)


def shards(queries, keys, values, attn, grad_out, w_out, starts):
    nseq = lax.axis_size("seq")
    seqlen = queries.shape[0] * nseq
    q_heads, k_heads, v_heads, o_heads = (
        lax.all_to_all(queries, "seq", split_axis=1, concat_axis=0, tiled=True),
        lax.all_to_all(keys, "seq", split_axis=1, concat_axis=0, tiled=True),
        lax.all_to_all(values, "seq", split_axis=1, concat_axis=0, tiled=True),
        lax.all_to_all(attn, "seq", split_axis=1, concat_axis=0, tiled=True),
    )
    local_w = q_heads.shape[1]
    heads_here = local_w // HDIM
    contract = (((1,), (1,)), ((), ()))
    full_grad = lax.all_gather(grad_out, "seq", axis=0, tiled=True)
    grad_attn = lax.dot_general(full_grad, w_out, contract, preferred_element_type=jnp.float32)
    partial_value = lax.dot_general(
        o_heads, full_grad, (((0,), (0,)), ((), ())), preferred_element_type=jnp.float32
    )
    grad_attn = grad_attn.astype(jnp.bfloat16)
    grad_w = lax.psum_scatter(
        partial_value.astype(jnp.bfloat16), "dp", scatter_dimension=1, tiled=True
    ).astype(jnp.float32)
    first = starts[0]
    positions = jnp.arange(seqlen)
    segment = jnp.max(jnp.where(first[None, :] <= positions[:, None], first[None, :], 0), axis=1)
    q_all = q_heads.reshape(seqlen, heads_here, HDIM)
    k_all = k_heads.reshape(seqlen, heads_here, HDIM)
    v_all = v_heads.reshape(seqlen, heads_here, HDIM)
    o_all = o_heads.reshape(seqlen, heads_here, HDIM)
    g_all = grad_attn.reshape(seqlen, heads_here, HDIM)
    scale = HDIM ** (-0.5)
    block = min(512, seqlen)
    nblocks = seqlen // block

    def step(carry, index):
        grad_keys_acc, grad_vals_acc = carry
        begin = index * block
        q_blk = lax.dynamic_slice_in_dim(q_all, begin, block, 0)
        g_blk = lax.dynamic_slice_in_dim(g_all, begin, block, 0)
        o_blk = lax.dynamic_slice_in_dim(o_all, begin, block, 0)
        pos_blk = begin + jnp.arange(block)
        seg_blk = lax.dynamic_slice_in_dim(segment, begin, block, 0)
        row_dot = jnp.sum(g_blk.astype(jnp.float32) * o_blk.astype(jnp.float32), axis=-1).T[
            :, :, None
        ]
        scores, live = tile_scores(q_blk, k_all, pos_blk, seg_blk, positions, scale)
        top = jnp.max(jnp.where(live, scores, -jnp.inf), axis=-1, keepdims=True)
        total = jnp.sum(jnp.where(live, jnp.exp(scores - top), 0.0), axis=-1, keepdims=True)
        grad_q, grad_k, grad_v = tile_grads(
            scores, live, top, total, q_blk, g_blk, row_dot, k_all, v_all
        )
        grad_keys_acc = grad_keys_acc + grad_k
        grad_vals_acc = grad_vals_acc + grad_v
        return ((grad_keys_acc, grad_vals_acc), grad_q)

    zero_kv = jnp.zeros((seqlen, heads_here, HDIM), jnp.float32)
    (grad_keys_all, grad_vals_all), grad_q_blocks = lax.scan(
        step, (zero_kv, zero_kv), jnp.arange(nblocks)
    )
    grad_q_heads = (grad_q_blocks.reshape(seqlen, local_w) * scale).astype(jnp.bfloat16)
    grad_k_heads = (grad_keys_all.reshape(seqlen, local_w) * scale).astype(jnp.bfloat16)
    grad_v_heads = grad_vals_all.reshape(seqlen, local_w).astype(jnp.bfloat16)
    grad_q_tok, grad_k_tok, grad_v_tok = (
        lax.all_to_all(grad_q_heads, "seq", split_axis=0, concat_axis=1, tiled=True),
        lax.all_to_all(grad_k_heads, "seq", split_axis=0, concat_axis=1, tiled=True),
        lax.all_to_all(grad_v_heads, "seq", split_axis=0, concat_axis=1, tiled=True),
    )
    return (grad_q_tok, grad_k_tok, grad_v_tok, grad_w)


def solution(mesh):
    in_specs = (
        P(("dp", "seq"), None),
        P(("dp", "seq"), None),
        P(("dp", "seq"), None),
        P(("dp", "seq"), None),
        P(("dp", "seq"), None),
        P("seq", None),
        P("dp", None),
    )
    out_specs = (
        P(("dp", "seq"), None),
        P(("dp", "seq"), None),
        P(("dp", "seq"), None),
        P("seq", "dp"),
    )
    return jax.shard_map(shards, mesh=mesh, in_specs=in_specs, out_specs=out_specs, check_vma=False)
```

profile of v0, /device:TPU:1, one launch (start us, length us, event | category | flops | bytes accessed | tf_op | source)
XLA Modules:
  0.0 266.7 jit_solution(2581469003296684086)
XLA Ops:
  7.2 0.7 all-gather.2.cloned.1.call-update
  7.9 2.0 copy.73
  10.0 7.6 %all-to-all-start = ((bf16[128,16,128]{0,2,1:T(8,128)(2,1)}), bf16[128,16,128]{0,2,1:T(8,128)(2,1)S(1)}, u32[]{:S(2)}, u32[]{:S(2)}) async-start(bf16[128,16,128]{0,2,1:T(8,128)(2,1)} %bitcast), calls=%async_computation | async-start | bytes 1048576 | tf_op jit(solution)/shard_map/all_to_all | solution.py:30
  17.6 2.0 copy.75
  19.6 8.3 %all-to-all-done = bf16[128,16,128]{0,2,1:T(8,128)(2,1)S(1)} async-done(((bf16[128,16,128]{0,2,1:T(8,128)(2,1)}), bf16[128,16,128]{0,2,1:T(8,128)(2,1)S(1)}, u32[]{:S(2)}, u32[]{:S(2)}) %all-to-all-start) | async-done | bytes 524320 | tf_op jit(solution)/shard_map/all_to_all | solution.py:30
  27.9 3.6 %all-to-all-start.1 = ((bf16[128,16,128]{0,2,1:T(8,128)(2,1)}), bf16[128,16,128]{0,2,1:T(8,128)(2,1)S(1)}, u32[]{:S(2)}, u32[]{:S(2)}) async-start(bf16[128,16,128]{0,2,1:T(8,128)(2,1)} %bitcast.4), calls=%async_computation.1 | async-start | bytes 1048576 | tf_op jit(solution)/shard_map/all_to_all | solution.py:31
  31.5 1.0 copy.77
  32.5 12.8 %all-to-all-done.1 = bf16[128,16,128]{0,2,1:T(8,128)(2,1)S(1)} async-done(((bf16[128,16,128]{0,2,1:T(8,128)(2,1)}), bf16[128,16,128]{0,2,1:T(8,128)(2,1)S(1)}, u32[]{:S(2)}, u32[]{:S(2)}) %all-to-all-start.1) | async-done | bytes 524320 | tf_op jit(solution)/shard_map/all_to_all | solution.py:31
  45.3 6.1 %all-to-all-start.2 = ((bf16[128,16,128]{0,2,1:T(8,128)(2,1)}), bf16[128,16,128]{0,2,1:T(8,128)(2,1)S(1)}, u32[]{:S(2)}, u32[]{:S(2)}) async-start(bf16[128,16,128]{0,2,1:T(8,128)(2,1)} %bitcast.8), calls=%async_computation.2 | async-start | bytes 1048576 | tf_op jit(solution)/shard_map/all_to_all | solution.py:32
  51.4 1.0 copy.79
  52.4 7.9 %all-to-all-done.2 = bf16[128,16,128]{0,2,1:T(8,128)(2,1)S(1)} async-done(((bf16[128,16,128]{0,2,1:T(8,128)(2,1)}), bf16[128,16,128]{0,2,1:T(8,128)(2,1)S(1)}, u32[]{:S(2)}, u32[]{:S(2)}) %all-to-all-start.2) | async-done | bytes 524320 | tf_op jit(solution)/shard_map/all_to_all | solution.py:32
  60.3 4.2 %all-to-all-start.3 = ((bf16[128,16,128]{0,2,1:T(8,128)(2,1)}), bf16[128,16,128]{0,2,1:T(8,128)(2,1)}, u32[]{:S(2)}, u32[]{:S(2)}) async-start(bf16[128,16,128]{0,2,1:T(8,128)(2,1)} %bitcast.11), calls=%async_computation.3 | async-start | bytes 1048576 | tf_op jit(solution)/shard_map/all_to_all | solution.py:33
  64.8 2.2 copy.74
  67.0 2.2 copy.76
  69.2 2.1 copy.78
  71.3 6.4 %all-to-all-done.3 = bf16[128,16,128]{0,2,1:T(8,128)(2,1)} async-done(((bf16[128,16,128]{0,2,1:T(8,128)(2,1)}), bf16[128,16,128]{0,2,1:T(8,128)(2,1)}, u32[]{:S(2)}, u32[]{:S(2)}) %all-to-all-start.3) | async-done | bytes 524320 | tf_op jit(solution)/shard_map/all_to_all | solution.py:33
  77.6 2.1 copy.80
  79.7 62.3 %all-gather.2.cloned.1.call-done = bf16[2048,4096]{1,0:T(8,128)(2,1)} async-done(((bf16[128,4096]{1,0:T(8,128)(2,1)}), bf16[2048,4096]{1,0:T(8,128)(2,1)}) %all-gather.2.cloned.1.call-update) | async-done | bytes 16777232 | tf_op jit(solution)/shard_map/all_gather | solution.py:38
  142.0 9.3 %convolution_convert_fusion = bf16[128,4096]{1,0:T(8,128)(2,1)} fusion(bf16[2048,128]{1,0:T(8,128)(2,1)} %bitcast.107, bf16[2048,4096]{1,0:T(8,128)(2,1)} %all-gather.2.cloned.1.call-done), kind=kOutput, calls=%fused_computation.34 | convolution fusion | flops 2148007936 | bytes 18350080 | tf_op jit(solution)/shard_map/dot_general | solution.py:40
  151.3 9.0 %fusion.25 = bf16[2048,1,128]{2,0,1:T(8,128)(2,1)} fusion(bf16[2048,4096]{1,0:T(8,128)(2,1)} %all-gather.2.cloned.1.call-done, bf16[128,4096]{1,0:T(8,128)(2,1)S(1)} %copy-done), kind=kOutput, calls=%fused_computation.36 | convolution fusion | flops 2147745792 | bytes 18350080 | tf_op jit(solution)/shard_map/dot_general | solution.py:39
  160.3 53.9 %while.16 = (s32[]{:T(128)}, f32[2048,1,128]{0,2,1:T(8,128)S(1)}, f32[2048,1,128]{0,2,1:T(8,128)S(1)}, f32[4,512,1,128]{3,1,2,0:T(8,128)}, s32[4]{0:T(128)S(1)},...) while((s32[]{:T(128)}, f32[2048,1,128]{0,2,1:T(8,128)S(1)}, ...), condition=%wide.region_5.6_spmd.clone.clone, body=%wide.region_1.5_spmd.clone.clone.sunk | while | flops 1368652800 | bytes 44597580 | solution.py:81
  161.5 1.1 multiply_reduce_fusion.2
  162.6 2.5 select_reduce_fusion.3
  165.2 1.9 fusion.53
  167.1 1.9 fusion.54
  170.1 0.7 multiply_convert_fusion.4
  170.9 1.5 fusion.55
  172.4 1.4 fusion.57
  175.0 1.1 multiply_reduce_fusion.2
  176.1 2.6 select_reduce_fusion.3
  178.7 1.9 fusion.53
  180.6 1.9 fusion.54
  183.6 0.7 multiply_convert_fusion.4
  184.4 1.5 fusion.55
  185.8 1.4 fusion.57
  188.5 1.1 multiply_reduce_fusion.2
  189.6 2.5 select_reduce_fusion.3
  192.1 1.9 fusion.53
  194.1 1.9 fusion.54
  197.1 0.7 multiply_convert_fusion.4
  197.8 1.5 fusion.55
  199.3 1.4 fusion.57
  201.9 1.1 multiply_reduce_fusion.2
  203.0 2.5 select_reduce_fusion.3
  205.6 1.9 fusion.53
  207.5 1.9 fusion.54
  210.5 0.7 multiply_convert_fusion.4
  211.2 1.5 fusion.55
  212.7 1.4 fusion.57
  214.2 2.1 multiply_convert_fusion.2
  216.3 5.0 %all-to-all-start.4 = ((bf16[16,128,128]{2,1,0:T(8,128)(2,1)}), bf16[16,128,128]{2,1,0:T(8,128)(2,1)}, u32[]{:S(2)}, u32[]{:S(2)}) async-start(bf16[16,128,128]{2,1,0:T(8,128)(2,1)} %bitcast.110), calls=%async_computation.4 | async-start | bytes 1048576 | tf_op jit(solution)/shard_map/all_to_all | solution.py:88
  221.3 0.9 multiply_convert_fusion.1
  222.2 2.0 copy.82
  224.2 7.4 %all-to-all-done.4 = bf16[16,128,128]{2,1,0:T(8,128)(2,1)} async-done(((bf16[16,128,128]{2,1,0:T(8,128)(2,1)}), bf16[16,128,128]{2,1,0:T(8,128)(2,1)}, u32[]{:S(2)}, u32[]{:S(2)}) %all-to-all-start.4) | async-done | bytes 524320 | tf_op jit(solution)/shard_map/all_to_all | solution.py:88
  231.7 3.7 %all-to-all-start.5 = ((bf16[16,128,128]{2,1,0:T(8,128)(2,1)}), bf16[16,128,128]{2,1,0:T(8,128)(2,1)S(1)}, u32[]{:S(2)}, u32[]{:S(2)}) async-start(bf16[16,128,128]{2,1,0:T(8,128)(2,1)} %bitcast.17), calls=%async_computation.5 | async-start | bytes 1048576 | tf_op jit(solution)/shard_map/all_to_all | solution.py:89
  235.4 1.0 copy.84
  236.4 8.2 %all-to-all-done.5 = bf16[16,128,128]{2,1,0:T(8,128)(2,1)S(1)} async-done(((bf16[16,128,128]{2,1,0:T(8,128)(2,1)}), bf16[16,128,128]{2,1,0:T(8,128)(2,1)S(1)}, u32[]{:S(2)}, u32[]{:S(2)}) %all-to-all-start.5) | async-done | bytes 524320 | tf_op jit(solution)/shard_map/all_to_all | solution.py:89
  244.6 3.6 %all-to-all-start.6 = ((bf16[16,128,128]{2,1,0:T(8,128)(2,1)}), bf16[16,128,128]{2,1,0:T(8,128)(2,1)S(1)}, u32[]{:S(2)}, u32[]{:S(2)}) async-start(bf16[16,128,128]{2,1,0:T(8,128)(2,1)} %bitcast.20), calls=%async_computation.6 | async-start | bytes 1048576 | tf_op jit(solution)/shard_map/all_to_all | solution.py:90
  248.1 1.3 copy.81
  249.5 1.0 copy.87
  250.8 1.0 copy.88
  251.8 5.3 %all-to-all-done.6 = bf16[16,128,128]{2,1,0:T(8,128)(2,1)S(1)} async-done(((bf16[16,128,128]{2,1,0:T(8,128)(2,1)}), bf16[16,128,128]{2,1,0:T(8,128)(2,1)S(1)}, u32[]{:S(2)}, u32[]{:S(2)}) %all-to-all-start.6) | async-done | bytes 524320 | tf_op jit(solution)/shard_map/all_to_all | solution.py:90
  257.3 1.0 copy.89
  258.4 1.5 convert_element_type.52
  (66 shorter events, 7.5 us)
Async XLA Ops:
  7.2 144.2 %copy-start = (bf16[128,4096]{1,0:T(8,128)(2,1)S(1)}, bf16[128,4096]{1,0:T(8,128)(2,1)}, u32[]{:S(2)}) copy-start(bf16[128,4096]{1,0:T(8,128)(2,1)} %param.14) | copy-start | bytes 3145732
  7.2 24.3 %copy-start.7 = (bf16[128,2048]{1,0:T(8,128)(2,1)S(1)}, bf16[128,2048]{1,0:T(8,128)(2,1)}, u32[]{:S(2)}) copy-start(bf16[128,2048]{1,0:T(8,128)(2,1)} %param.11) | copy-start | bytes 1572868
  7.2 44.2 %copy-start.8 = (bf16[128,2048]{1,0:T(8,128)(2,1)S(1)}, bf16[128,2048]{1,0:T(8,128)(2,1)}, u32[]{:S(2)}) copy-start(bf16[128,2048]{1,0:T(8,128)(2,1)} %param.12) | copy-start | bytes 1572868
  7.2 134.8 %all-gather.2.cloned.1.call-start = ((), (), s32[]{:S(2)}) async-start(), calls=%async_computation.8 | async-start | bytes 17825792 | tf_op jit(solution)/shard_map/all_gather | solution.py:38
  7.9 56.8 %copy-start.9 = (s32[1,8]{1,0:T(1,128)S(1)}, s32[1,8]{1,0:T(1,128)}, u32[]{:S(2)}) copy-start(s32[1,8]{1,0:T(1,128)} %param.15) | copy-start | bytes 100
  10.0 17.9 %all-to-all-start = ((bf16[128,16,128]{0,2,1:T(8,128)(2,1)}), bf16[128,16,128]{0,2,1:T(8,128)(2,1)S(1)}, u32[]{:S(2)}, u32[]{:S(2)}) async-start(bf16[128,16,128]{0,2,1:T(8,128)(2,1)} %bitcast), calls=%async_computation | async-start | bytes 1048576 | tf_op jit(solution)/shard_map/all_to_all | solution.py:30
  27.9 36.7 %copy-start.4 = (bf16[128,16,128]{0,2,1:T(8,128)(2,1)}, bf16[128,16,128]{0,2,1:T(8,128)(2,1)S(1)}, u32[]{:S(2)}) copy-start(bf16[128,16,128]{0,2,1:T(8,128)(2,1)S(1)} %all-to-all-done) | copy-start | bytes 1572868
  27.9 17.4 %all-to-all-start.1 = ((bf16[128,16,128]{0,2,1:T(8,128)(2,1)}), bf16[128,16,128]{0,2,1:T(8,128)(2,1)S(1)}, u32[]{:S(2)}, u32[]{:S(2)}) async-start(bf16[128,16,128]{0,2,1:T(8,128)(2,1)} %bitcast.4), calls=%async_computation.1 | async-start | bytes 1048576 | tf_op jit(solution)/shard_map/all_to_all | solution.py:31
  45.3 19.4 %copy-start.5 = (bf16[128,16,128]{0,2,1:T(8,128)(2,1)}, bf16[128,16,128]{0,2,1:T(8,128)(2,1)S(1)}, u32[]{:S(2)}) copy-start(bf16[128,16,128]{0,2,1:T(8,128)(2,1)S(1)} %all-to-all-done.1) | copy-start | bytes 1572868
  45.3 15.1 %all-to-all-start.2 = ((bf16[128,16,128]{0,2,1:T(8,128)(2,1)}), bf16[128,16,128]{0,2,1:T(8,128)(2,1)S(1)}, u32[]{:S(2)}, u32[]{:S(2)}) async-start(bf16[128,16,128]{0,2,1:T(8,128)(2,1)} %bitcast.8), calls=%async_computation.2 | async-start | bytes 1048576 | tf_op jit(solution)/shard_map/all_to_all | solution.py:32
  60.3 4.3 %copy-start.6 = (bf16[128,16,128]{0,2,1:T(8,128)(2,1)}, bf16[128,16,128]{0,2,1:T(8,128)(2,1)S(1)}, u32[]{:S(2)}) copy-start(bf16[128,16,128]{0,2,1:T(8,128)(2,1)S(1)} %all-to-all-done.2) | copy-start | bytes 1572868
  60.3 17.3 %all-to-all-start.3 = ((bf16[128,16,128]{0,2,1:T(8,128)(2,1)}), bf16[128,16,128]{0,2,1:T(8,128)(2,1)}, u32[]{:S(2)}, u32[]{:S(2)}) async-start(bf16[128,16,128]{0,2,1:T(8,128)(2,1)} %bitcast.11), calls=%async_computation.3 | async-start | bytes 1048576 | tf_op jit(solution)/shard_map/all_to_all | solution.py:33
  64.6 193.8 %reduce-scatter.2.cloned.1.call-start = ((), (), s32[]{:S(2)}) async-start(), calls=%async_computation.9 | async-start | bytes 1114112 | tf_op jit(solution)/shard_map/reduce_scatter | solution.py:44
  167.1 2.0 copy-start.3
  169.1 1.0 copy-start.2
  170.1 2.2 copy-start.1
  180.6 2.0 copy-start.3
  182.6 1.0 copy-start.2
  183.6 2.2 copy-start.1
  194.0 2.0 copy-start.3
  196.0 1.0 copy-start.2
  197.1 2.2 copy-start.1
  207.5 2.0 copy-start.3
  209.5 1.0 copy-start.2
  210.5 2.2 copy-start.1
  216.3 15.4 %all-to-all-start.4 = ((bf16[16,128,128]{2,1,0:T(8,128)(2,1)}), bf16[16,128,128]{2,1,0:T(8,128)(2,1)}, u32[]{:S(2)}, u32[]{:S(2)}) async-start(bf16[16,128,128]{2,1,0:T(8,128)(2,1)} %bitcast.110), calls=%async_computation.4 | async-start | bytes 1048576 | tf_op jit(solution)/shard_map/all_to_all | solution.py:88
  231.7 12.9 %all-to-all-start.5 = ((bf16[16,128,128]{2,1,0:T(8,128)(2,1)}), bf16[16,128,128]{2,1,0:T(8,128)(2,1)S(1)}, u32[]{:S(2)}, u32[]{:S(2)}) async-start(bf16[16,128,128]{2,1,0:T(8,128)(2,1)} %bitcast.17), calls=%async_computation.5 | async-start | bytes 1048576 | tf_op jit(solution)/shard_map/all_to_all | solution.py:89
  244.6 12.5 %all-to-all-start.6 = ((bf16[16,128,128]{2,1,0:T(8,128)(2,1)}), bf16[16,128,128]{2,1,0:T(8,128)(2,1)S(1)}, u32[]{:S(2)}, u32[]{:S(2)}) async-start(bf16[16,128,128]{2,1,0:T(8,128)(2,1)} %bitcast.20), calls=%async_computation.6 | async-start | bytes 1048576 | tf_op jit(solution)/shard_map/all_to_all | solution.py:90
Sparse Core Ops, SparseCore 0:
  10.5 131.4 all-gather.1
  151.5 54.0 reduce-scatter.1
where the time goes:
time: 271 us; the launch traced here: 267 us
  waiting for transfers between devices  119 us (44%)
  matrix products  45.2 us (17%)
  starting transfers between devices  33.8 us (12%)
  local copies, waits for them, and re-layouts  27 us (10%)
  other arithmetic  24.7 us (9%)
  between operations  14.2 us (5%)
    all_gather x1, waiting for transfers between devices, shards(): full_grad = lax.all_gather(grad_out, 'seq', axis=0, tiled=True)  62.3 us
    all_to_all x1, waiting for transfers between devices, shards(): lax.all_to_all(keys, 'seq', split_axis=1, concat_axis=0, tiled=True)  12.8 us
    dot_general x4, matrix products, tile_scores(): jnp.einsum('qhd,khd->hqk', q_blk, key_tile, preferred_element_type=jnp.fl...  10.2 us
    dot_general x1, matrix products, shards(): lax.dot_general(o_heads, full_grad, (((0,), (0,)), ((), ())), preferred_e...  9.31 us
    unnamed x21, local copies, waits for them, and re-layouts  9.17 us
    dot_general x1, matrix products, shards(): lax.dot_general(full_grad, w_out, contract, preferred_element_type=jnp.fl...  8.97 us
    all_to_all x1, waiting for transfers between devices, shards(): lax.all_to_all(queries, 'seq', split_axis=1, concat_axis=0, tiled=True)  8.26 us
    all_to_all x1, waiting for transfers between devices, shards(): lax.all_to_all(grad_k_heads, 'seq', split_axis=0, concat_axis=1, tiled=True)  8.15 us
  transfers between devices with their start and end apart: 9, of which 8 were waited for; matrix products, arithmetic and copies ran while one was open for 32% of the time, Pallas kernels for 0%

commit v1 on v0

v1 whole, which is shorter than its diff:
```python
import functools

import jax
import jax.numpy as jnp
from jax import lax
from jax.experimental import pallas as pl
from jax.experimental.pallas import tpu as pltpu
from jax.sharding import PartitionSpec as P

HDIM = 128
MESH = pl.DeviceIdType.MESH
BF16 = jnp.bfloat16
F32 = jnp.float32
NT = (((1,), (1,)), ((), ()))
NN = (((1,), (0,)), ((), ()))
TN = (((0,), (0,)), ((), ()))
VMEM_LIMIT = 56 << 20


def place():
    dp = lax.axis_index("dp")
    s = lax.axis_index("seq")
    c = dp % 2
    x, y = s // 4, s % 4
    p = x * (1 - c) + y * c
    q = y * (1 - c) + x * c
    sp, sq = 4 - 3 * c, 1 + 3 * c

    def block(pp, qq):
        return pp * sp + qq * sq

    return dp, c, s, p, q, block


def remote(src, dst, ssem, rsem, dp, s):
    cp = pltpu.make_async_remote_copy(
        src_ref=src, dst_ref=dst, send_sem=ssem, recv_sem=rsem, device_id=(dp, s), device_id_type=MESH
    )
    cp.start()


def drain(ref, sem):
    pltpu.make_async_copy(ref, ref, sem).wait()


def rows(i, n=128):
    return pl.ds(pl.multiple_of(i * n, n), n)


def gather_kernel(
    q_in, k_in, v_in, o_in, g_in, w_in,
    qh, kh, vh, gh, rdh, dwp,
    gbuf, wbuf, abuf, atbuf, gsnd, rdsnd, dwv,
    g_rs, w_rs, a_rs, h_rs, ga_rs, rd_rs,
    g_ss, w_ss, a_ss, h_ss, ga_ss, rd_ss, loc, dw_sem,
):
    dp, c, s, p, q, block = place()
    bar = pltpu.get_barrier_semaphore()
    for a in range(4):
        for b in range(4):
            if a or b:
                pl.semaphore_signal(
                    bar, 1, device_id=(dp, block((p + a) % 4, (q + b) % 4)), device_id_type=MESH
                )

    lg = pltpu.make_async_copy(g_in, gbuf.at[rows(q)], loc.at[0])
    lw = pltpu.make_async_copy(w_in, wbuf.at[rows(p)], loc.at[1])
    lg.start()
    lw.start()
    la = []
    for pp in range(4):
        cp = pltpu.make_async_copy(
            o_in.at[:, rows(block(pp, q))], abuf.at[rows(q), pl.ds(pp * 128, 128)], loc.at[2 + pp]
        )
        cp.start()
        la.append(cp)
    lh = []
    for t, (src, dst) in enumerate(((q_in, qh), (k_in, kh), (v_in, vh))):
        cp = pltpu.make_async_copy(src.at[:, rows(s)], dst.at[rows(s)], loc.at[6 + t])
        cp.start()
        lh.append(cp)

    pl.semaphore_wait(bar, 15)
    for b in (1, 3, 2):
        qq = (q + b) % 4
        remote(g_in, gbuf.at[rows(q)], g_ss, g_rs.at[q], dp, block(p, qq))
        pp = (p + b) % 4
        remote(w_in, wbuf.at[rows(p)], w_ss, w_rs.at[p], dp, block(pp, q))
        for f in range(4):
            remote(
                o_in.at[:, rows(block(f, qq))], abuf.at[rows(q), pl.ds(f * 128, 128)], a_ss, a_rs, dp, block(p, qq)
            )

    lg.wait()
    lw.wait()
    for cp in la:
        cp.wait()
    for b in (1, 3, 2):
        qq = (q + b) % 4
        drain(gbuf.at[rows(qq)], g_rs.at[qq])
        pp = (p + b) % 4
        drain(wbuf.at[rows(pp)], w_rs.at[pp])
    drain(abuf.at[pl.ds(0, 384)], a_rs)

    for a in range(4):
        for b in range(4):
            if a or b:
                d = block((p + a) % 4, (q + b) % 4)
                for t, (src, dst) in enumerate(((q_in, qh), (k_in, kh), (v_in, vh))):
                    remote(src.at[:, rows(d)], dst.at[rows(s)], h_ss.at[t], h_rs.at[t], dp, d)

    ones = jnp.ones((8, 128), F32)
    for n in range(2):
        ga = lax.dot_general(
            gbuf[...], wbuf[pl.ds(n * 256, 256), :], NT, preferred_element_type=F32
        ).astype(BF16)
        for m in range(2):
            f = n * 2 + m
            gf = ga[:, m * 128 : (m + 1) * 128]
            gsnd[f] = gf
            prod = gf.astype(F32) * abuf[:, f * 128 : (f + 1) * 128].astype(F32)
            rd = lax.dot_general(ones, prod, NT, preferred_element_type=F32, precision=lax.Precision.HIGHEST)
            for t in range(4):
                rdsnd[f, t] = rd[:, t * 128 : (t + 1) * 128]

    lga = []
    for b in range(4):
        cp = pltpu.make_async_copy(gsnd.at[p, pl.ds(b * 128, 128)], gh.at[rows(block(p, b))], loc.at[9 + b])
        cp.start()
        lga.append(cp)
        cp = pltpu.make_async_copy(rdsnd.at[p, b], rdh.at[block(p, b)], loc.at[13 + b])
        cp.start()
        lga.append(cp)
    for a in (1, 3, 2):
        pp = (p + a) % 4
        for b in range(4):
            remote(gsnd.at[pp, pl.ds(b * 128, 128)], gh.at[rows(block(p, b))], ga_ss, ga_rs, dp, block(pp, q))
            remote(rdsnd.at[pp, b], rdh.at[block(p, b)], rd_ss, rd_rs, dp, block(pp, q))

    atbuf[...] = abuf[...].T

    @pl.loop(0, 8)
    def _(n):
        cols = rows(n, 512)
        dwv[:, cols] = lax.dot_general(
            atbuf[...], gbuf[:, cols], NN, preferred_element_type=F32
        ).astype(BF16)

    cdw = pltpu.make_async_copy(dwv, dwp, dw_sem)
    cdw.start()

    for cp in lga:
        cp.wait()
    for cp in lh:
        cp.wait()
    drain(gsnd.at[pl.ds(0, 3)], ga_rs)
    drain(rdsnd.at[pl.ds(0, 3)], rd_rs)
    for t, dst in enumerate((qh, kh, vh)):
        drain(dst.at[pl.ds(0, 1920)], h_rs.at[t])
    cdw.wait()
    drain(gbuf.at[pl.ds(0, 384)], g_ss)
    drain(wbuf.at[pl.ds(0, 384)], w_ss)
    drain(abuf.at[pl.ds(0, 384)], a_ss)
    drain(gsnd.at[pl.ds(0, 3)], ga_ss)
    drain(rdsnd.at[pl.ds(0, 3)], rd_ss)
    for t, dst in enumerate((qh, kh, vh)):
        drain(dst.at[pl.ds(0, 1920)], h_ss.at[t])


def gather(queries, keys, values, attn, grad_out, w_out):
    any_ = pl.BlockSpec(memory_space=pl.ANY)
    head = jax.ShapeDtypeStruct((2048, 128), BF16)
    dma = pltpu.SemaphoreType.DMA
    return pl.pallas_call(
        gather_kernel,
        out_shape=(head, head, head, head, jax.ShapeDtypeStruct((16, 8, 128), F32),
                   jax.ShapeDtypeStruct((512, 4096), BF16)),
        in_specs=[any_] * 6,
        out_specs=(any_,) * 6,
        scratch_shapes=[
            pltpu.VMEM((512, 4096), BF16), pltpu.VMEM((512, 4096), BF16), pltpu.VMEM((512, 512), BF16),
            pltpu.VMEM((512, 512), BF16), pltpu.VMEM((4, 512, 128), BF16), pltpu.VMEM((4, 4, 8, 128), F32),
            pltpu.VMEM((512, 4096), BF16),
            dma((4,)), dma((4,)), dma, dma((3,)), dma, dma,
            dma, dma, dma, dma((3,)), dma, dma, dma((17,)), dma,
        ],
        compiler_params=pltpu.CompilerParams(collective_id=0, has_side_effects=True, vmem_limit_bytes=VMEM_LIMIT),
        name="gather_project",
    )(queries, keys, values, attn, grad_out, w_out)


BLK = 512
SCALE = HDIM ** (-0.5)
LOG2E = 1.4426950408889634


def attn_kernel(first, q, k, v, g, rd, dq, dk, dv, sbuf, dka, dva):
    dka[...] = jnp.zeros_like(dka)
    dva[...] = jnp.zeros_like(dva)
    nb = 2048 // BLK
    for i in range(nb):
        qs = pl.ds(i * BLK, BLK)
        pos = lax.broadcasted_iota(jnp.int32, (1, BLK), 1) + i * BLK
        seg = jnp.zeros((1, BLK), jnp.int32)
        low = jnp.int32(0)
        for e in range(8):
            st = first[0, e]
            seg = jnp.where(pos >= st, jnp.maximum(seg, st), seg)
            low = jnp.where(st <= i * BLK, jnp.maximum(low, st), low)
        jmin = low // BLK
        rdi = jnp.concatenate([rd[i * (BLK // 128) + t][:1] for t in range(BLK // 128)], axis=1)

        def scores(j, m):
            ks = pl.ds(pl.multiple_of(j * BLK, BLK), BLK)
            sc = lax.dot_general(k[ks, :], q[qs, :], NT, preferred_element_type=F32) * (SCALE * LOG2E)
            kp = lax.broadcasted_iota(jnp.int32, (BLK, BLK), 0) + j * BLK
            sc = jnp.where((kp <= pos) & (kp >= seg), sc, -1e30)
            sbuf[ks, :] = sc
            return jnp.maximum(m, jnp.max(sc.reshape(BLK // 8, 8, BLK), axis=0))

        m = lax.fori_loop(jmin, i + 1, scores, jnp.full((8, BLK), -1e30, F32))
        m = jnp.max(m, axis=0, keepdims=True)

        def expo(j, tot):
            ks = pl.ds(pl.multiple_of(j * BLK, BLK), BLK)
            e = jnp.exp2(sbuf[ks, :] - m)
            sbuf[ks, :] = e
            return tot + jnp.sum(e.reshape(BLK // 8, 8, BLK), axis=0)

        tot = lax.fori_loop(jmin, i + 1, expo, jnp.zeros((8, BLK), F32))
        inv = 1.0 / jnp.sum(tot, axis=0, keepdims=True)

        def grads(j, acc):
            ks = pl.ds(pl.multiple_of(j * BLK, BLK), BLK)
            prob = sbuf[ks, :] * inv
            gp = lax.dot_general(v[ks, :], g[qs, :], NT, preferred_element_type=F32)
            ds = (prob * (gp - rdi)).astype(BF16)
            dva[ks, :] += lax.dot_general(prob.astype(BF16), g[qs, :], NN, preferred_element_type=F32)
            dka[ks, :] += lax.dot_general(ds, q[qs, :], NN, preferred_element_type=F32)
            return acc + lax.dot_general(ds, k[ks, :], TN, preferred_element_type=F32)

        acc = lax.fori_loop(jmin, i + 1, grads, jnp.zeros((BLK, HDIM), F32))
        dq[qs, :] = (acc * SCALE).astype(BF16)
    dk[...] = (dka[...] * SCALE).astype(BF16)
    dv[...] = dva[...].astype(BF16)


def attention(first, q, k, v, g, rd):
    vm = pl.BlockSpec(memory_space=pltpu.VMEM)
    head = jax.ShapeDtypeStruct((2048, 128), BF16)
    return pl.pallas_call(
        attn_kernel,
        out_shape=(head, head, head),
        in_specs=[pl.BlockSpec(memory_space=pltpu.SMEM)] + [vm] * 5,
        out_specs=(vm,) * 3,
        scratch_shapes=[pltpu.VMEM((2048, BLK), F32), pltpu.VMEM((2048, HDIM), F32), pltpu.VMEM((2048, HDIM), F32)],
        compiler_params=pltpu.CompilerParams(vmem_limit_bytes=VMEM_LIMIT),
        name="attention_grads",
    )(first, q, k, v, g, rd)


def return_kernel(
    dq, dk, dv, dwp, oq, ok, ov, ow, pbuf, psum, zbuf, h_rs, p_rs, z_rs, h_ss, p_ss, z_ss, loc,
):
    dp, c, s, p, q, block = place()
    bar = pltpu.get_barrier_semaphore()
    for a in range(4):
        for b in range(4):
            if a or b:
                pl.semaphore_signal(
                    bar, 1, device_id=(dp, block((p + a) % 4, (q + b) % 4)), device_id_type=MESH
                )
    for a in range(1, 16):
        pl.semaphore_signal(bar, 1, device_id=((dp + a) % 16, s), device_id_type=MESH)
    lp = pltpu.make_async_copy(dwp.at[rows(p)], pbuf.at[p], loc.at[0])
    lp.start()
    lh = []
    for t, (src, dst) in enumerate(((dq, oq), (dk, ok), (dv, ov))):
        cp = pltpu.make_async_copy(src.at[rows(s)], dst.at[:, rows(s)], loc.at[1 + t])
        cp.start()
        lh.append(cp)
    pl.semaphore_wait(bar, 30)
    for a in (1, 3, 2):
        pp = (p + a) % 4
        remote(dwp.at[rows(pp)], pbuf.at[p], p_ss, p_rs, dp, block(pp, q))
    lp.wait()
    drain(pbuf.at[pl.ds(0, 3)], p_rs)
    for a in range(4):
        for b in range(4):
            if a or b:
                d = block((p + a) % 4, (q + b) % 4)
                for t, (src, dst) in enumerate(((dq, oq), (dk, ok), (dv, ov))):
                    remote(src.at[rows(d)], dst.at[:, rows(s)], h_ss.at[t], h_rs.at[t], dp, d)
    for n in range(16):
        cs = slice(n * 256, (n + 1) * 256)
        tot = pbuf[0, :, cs].astype(F32)
        for a in range(1, 4):
            tot += pbuf[a, :, cs].astype(F32)
        psum[n] = tot.astype(BF16)
    lz = pltpu.make_async_copy(psum.at[dp], zbuf.at[dp], loc.at[4])
    lz.start()
    for a in range(1, 16):
        d = (dp + a) % 16
        remote(psum.at[d], zbuf.at[dp], z_ss, z_rs, d, s)
    lz.wait()
    drain(zbuf.at[pl.ds(0, 15)], z_rs)
    tot = zbuf[0].astype(F32)
    for n in range(1, 16):
        tot += zbuf[n].astype(F32)
    ow[...] = tot
    for cp in lh:
        cp.wait()
    for t, src in enumerate((dq, dk, dv)):
        drain(src.at[pl.ds(0, 1920)], h_rs.at[t])
    drain(pbuf.at[pl.ds(0, 3)], p_ss)
    drain(zbuf.at[pl.ds(0, 15)], z_ss)
    for t, src in enumerate((dq, dk, dv)):
        drain(src.at[pl.ds(0, 1920)], h_ss.at[t])


def give_back(dq, dk, dv, dwp):
    any_ = pl.BlockSpec(memory_space=pl.ANY)
    tok = jax.ShapeDtypeStruct((128, 2048), BF16)
    dma = pltpu.SemaphoreType.DMA
    return pl.pallas_call(
        return_kernel,
        out_shape=(tok, tok, tok, jax.ShapeDtypeStruct((128, 256), F32)),
        in_specs=[any_] * 4,
        out_specs=(any_, any_, any_, pl.BlockSpec(memory_space=pltpu.VMEM)),
        scratch_shapes=[
            pltpu.VMEM((4, 128, 4096), BF16), pltpu.VMEM((16, 128, 256), BF16), pltpu.VMEM((16, 128, 256), BF16),
            dma((3,)), dma, dma, dma((3,)), dma, dma, dma((5,)),
        ],
        compiler_params=pltpu.CompilerParams(collective_id=1, has_side_effects=True, vmem_limit_bytes=VMEM_LIMIT),
        name="return_reduce",
    )(dq, dk, dv, dwp)


def shards(queries, keys, values, attn, grad_out, w_out, starts):
    qh, kh, vh, gh, rdh, dwp = gather(queries, keys, values, attn, grad_out, w_out)
    dq, dk, dv = attention(starts, qh, kh, vh, gh, rdh)
    return give_back(dq, dk, dv, dwp)


def solution(mesh):
    tok = P(("dp", "seq"), None)
    return jax.shard_map(
        shards,
        mesh=mesh,
        in_specs=(tok, tok, tok, tok, tok, P("seq", None), P("dp", None)),
        out_specs=(tok, tok, tok, P("seq", "dp")),
        check_vma=False,
    )
```

time: 271 us -> 162 us (0.60); the launches traced: 267 us -> 161 us
  Pallas kernels: 0 us -> 154 us
  waiting for transfers between devices: 119 us -> 0 us
  matrix products: 45.2 us -> 0 us
  starting transfers between devices: 33.8 us -> 0 us
  other arithmetic: 24.7 us -> 0 us
  local copies, waits for them, and re-layouts: 27 us -> 7.21 us
  between operations: 14.2 us -> 0.65 us
    pallas_call x0 -> x3, Pallas kernels: none -> 154 us  [the longest x1 79.8 us: gather(): pl.pallas_call(gather_kernel, out_shape=(head, head, head, head, jax.Shap...]
    all_gather x1 -> x0, waiting for transfers between devices: 62.3 us -> none  [shards(): full_grad = lax.all_gather(grad_out, 'seq', axis=0, tiled=True)]
    all_to_all x7 -> x0, waiting for transfers between devices: 56.2 us -> none  [the longest x1 12.8 us: shards(): lax.all_to_all(keys, 'seq', split_axis=1, concat_axis=0, tiled=True)]
    dot_general x22 -> x0, matrix products: 45.2 us -> none  [the longest x4 10.2 us: tile_scores(): jnp.einsum('qhd,khd->hqk', q_blk, key_tile, preferred_element_type=jnp.fl...]
    all_to_all x7 -> x0, starting transfers between devices: 33.7 us -> none  [the longest x1 7.58 us: shards(): lax.all_to_all(queries, 'seq', split_axis=1, concat_axis=0, tiled=True)]
    reduce_sum x8 -> x0, other arithmetic: 12.2 us -> none  [the longest x4 7.76 us: step(): jnp.sum(jnp.where(live, jnp.exp(scores - top), 0.0), axis=-1, keepdims=True)]
    all_to_all x7 -> x0, local copies, waits for them, and re-layouts: 10.4 us -> none  [the longest x1 2.2 us: shards(): lax.all_to_all(queries, 'seq', split_axis=1, concat_axis=0, tiled=True)]
    div x4 -> x0, other arithmetic: 7.75 us -> none  [tile_grads(): prob = jnp.where(live, jnp.exp(scores - top), 0.0) / total]
  transfers between devices with their start and end apart: 9 -> 0, of which waited for: 8 -> 0; matrix products, arithmetic and copies ran while one was open for 32% -> 0% of each run, Pallas kernels for 0% -> 0%
where the time goes in v1:
time: 162 us; the launch traced here: 161 us
  Pallas kernels  154 us (95%)
  local copies, waits for them, and re-layouts  7.21 us (4%)
    pallas_call x1, Pallas kernels, gather(): pl.pallas_call(gather_kernel, out_shape=(head, head, head, head, jax.Shap...  79.8 us
    pallas_call x1, Pallas kernels, give_back(): pl.pallas_call(return_kernel, out_shape=(tok, tok, tok, jax.ShapeDtypeStr...  60.5 us
    pallas_call x1, Pallas kernels, attention(): pl.pallas_call(attn_kernel, out_shape=(head, head, head), in_specs=[pl.Bl...  13.3 us
    unnamed x4, local copies, waits for them, and re-layouts  7.21 us

profile of v1, /device:TPU:1, one launch (start us, length us, event | category | flops | bytes accessed | tf_op | source)
XLA Modules:
  0.0 161.4 jit_solution(4047210150370842401)
XLA Ops:
  0.6 79.8 %gather_project.1 = (bf16[2048,128]{1,0:T(8,128)(2,1)}, bf16[2048,128]{1,0:T(8,128)(2,1)}, bf16[2048,128]{1,0:T(8,128)(2,1)}, bf16[2048,128]{1,0:T(8,128)(2,1)},...) custom-call(bf16[128,2048]{1,0:T(8,128)(2,1)} %q_in.1, bf16[128,2048]{1,0:T(8,128)(2,1)} %k_in.1, ...), custom_call_target="tpu_custom_call" | custom-call | tf_op jit(solution)/shard_map/gather_project/pallas_call | solution.py:174
  80.4 13.3 %attention_grads.1 = (bf16[2048,128]{1,0:T(8,128)(2,1)}, bf16[2048,128]{1,0:T(8,128)(2,1)}, bf16[2048,128]{1,0:T(8,128)(2,1)}) custom-call(s32[1,8]{1,0:T(1,128)} %first.1, bf16[2048,128]{1,0:T(8,128)(2,1)} %get-tuple-element.13.q, bf16[2048,128]{1,0:T(8,128)(2,1)} %get-tuple-element.14.k, bf16[2048,128]{1,0:T(8,128)(2,1)} %get-tuple-element.15.v, ...), custom_call_target="tpu_custom_call" | custom-call | tf_op jit(solution)/shard_map/attention_grads/pallas_call | solution.py:251
  93.8 60.5 %return_reduce.1 = (bf16[128,2048]{1,0:T(8,128)(2,1)}, bf16[128,2048]{1,0:T(8,128)(2,1)}, bf16[128,2048]{1,0:T(8,128)(2,1)}, f32[128,256]{1,0:T(8,128)}) custom-call(bf16[2048,128]{1,0:T(8,128)(2,1)} %get-tuple-element.18.dq, bf16[2048,128]{1,0:T(8,128)(2,1)} %get-tuple-element.19.dk, bf16[2048,128]{1,0:T(8,128)(2,1)} %get-tuple-element.20.dv, ...), custom_call_target="tpu_custom_call" | custom-call | tf_op jit(solution)/shard_map/return_reduce/pallas_call | solution.py:325
  154.2 1.9 %copy.15 = bf16[128,2048]{1,0:T(8,128)(2,1)} copy(bf16[128,2048]{1,0:T(8,128)(2,1)} %get-tuple-element.26) | data formatting | bytes 1048576
  156.1 1.9 %copy.16 = bf16[128,2048]{1,0:T(8,128)(2,1)} copy(bf16[128,2048]{1,0:T(8,128)(2,1)} %get-tuple-element.27) | data formatting | bytes 1048576
  158.0 1.9 %copy.17 = bf16[128,2048]{1,0:T(8,128)(2,1)} copy(bf16[128,2048]{1,0:T(8,128)(2,1)} %get-tuple-element.28) | data formatting | bytes 1048576
  159.9 1.6 copy.18

commit v2 on v1

--- a/solution.py
+++ b/solution.py
@@ -47,14 +47,46 @@
     return pl.ds(pl.multiple_of(i * n, n), n)
 
 
+STEPS = 5
+
+
+def spread(src, buf, me, send, ss, rs):
+    nxt, prv = (me + 1) % 4, (me + 3) % 4
+    top, low = src.at[pl.ds(0, 64)], src.at[pl.ds(64, 64)]
+    send(top, buf.at[rows(me * 2, 64)], ss, rs.at[0], nxt)
+    send(low, buf.at[rows(me * 2 + 1, 64)], ss, rs.at[1], prv)
+    send(low, buf.at[rows(me * 2 + 1, 64)], ss, rs.at[2], nxt)
+    send(top, buf.at[rows(me * 2, 64)], ss, rs.at[3], prv)
+
+
+def pass_on(buf, me, send, ss, rs):
+    nxt, prv = (me + 1) % 4, (me + 3) % 4
+    top = buf.at[rows(prv * 2, 64)]
+    drain(top, rs.at[0])
+    send(top, top, ss, rs.at[4], nxt)
+    low = buf.at[rows(nxt * 2 + 1, 64)]
+    drain(low, rs.at[1])
+    send(low, low, ss, rs.at[5], prv)
+
+
+def arrive(buf, me, rs):
+    nxt, prv, opp = (me + 1) % 4, (me + 3) % 4, (me + 2) % 4
+    drain(buf.at[rows(prv * 2 + 1, 64)], rs.at[2])
+    drain(buf.at[rows(nxt * 2, 64)], rs.at[3])
+    drain(buf.at[rows(opp * 2, 64)], rs.at[4])
+    drain(buf.at[rows(opp * 2 + 1, 64)], rs.at[5])
+
+
 def gather_kernel(
     q_in, k_in, v_in, o_in, g_in, w_in,
-    qh, kh, vh, gh, rdh, dwp,
-    gbuf, wbuf, abuf, atbuf, gsnd, rdsnd, dwv,
-    g_rs, w_rs, a_rs, h_rs, ga_rs, rd_rs,
-    g_ss, w_ss, a_ss, h_ss, ga_ss, rd_ss, loc, dw_sem,
+    qh, kh, vh, gh, rdh, cur, own,
+    gbuf, wbuf, abuf, atbuf, gsnd, rdsnd, dwv, slots,
+    g_rs, w_rs, a_rs, h_rs, ga_rs, rd_rs, r_rs,
+    g_ss, w_ss, a_ss, h_ss, ga_ss, rd_ss, r_ss, loc,
 ):
     dp, c, s, p, q, block = place()
+    z = dp // 2
+    up, down = ((z + 1) % 8) * 2 + c, ((z + 7) % 8) * 2 + c
     bar = pltpu.get_barrier_semaphore()
     for a in range(4):
         for b in range(4):
@@ -62,6 +94,8 @@
                 pl.semaphore_signal(
                     bar, 1, device_id=(dp, block((p + a) % 4, (q + b) % 4)), device_id_type=MESH
                 )
+    pl.semaphore_signal(bar, 1, device_id=(up, s), device_id_type=MESH)
+    pl.semaphore_signal(bar, 1, device_id=(down, s), device_id_type=MESH)
 
     lg = pltpu.make_async_copy(g_in, gbuf.at[rows(q)], loc.at[0])
     lw = pltpu.make_async_copy(w_in, wbuf.at[rows(p)], loc.at[1])
@@ -74,40 +108,76 @@
         )
         cp.start()
         la.append(cp)
+    heads = ((q_in, qh), (k_in, kh), (v_in, vh))
     lh = []
-    for t, (src, dst) in enumerate(((q_in, qh), (k_in, kh), (v_in, vh))):
+    for t, (src, dst) in enumerate(heads):
         cp = pltpu.make_async_copy(src.at[:, rows(s)], dst.at[rows(s)], loc.at[6 + t])
         cp.start()
         lh.append(cp)
 
-    pl.semaphore_wait(bar, 15)
+    def send_q(src, dst, ssem, rsem, qq):
+        remote(src, dst, ssem, rsem, dp, block(p, qq))
+
+    def send_p(src, dst, ssem, rsem, pp):
+        remote(src, dst, ssem, rsem, dp, block(pp, q))
+
+    def send_heads(t):
+        src, dst = heads[t]
+        for a in range(4):
+            for b in range(4):
+                if a or b:
+                    d = block((p + a) % 4, (q + b) % 4)
+                    remote(src.at[:, rows(d)], dst.at[rows(s)], h_ss.at[t], h_rs.at[t], dp, d)
+
+    def ring_send(t):
+        for lane in range(4):
+            src = dwv.at[0, lane] if t == 0 else slots.at[t - 1, lane]
+            remote(src, slots.at[t, lane], r_ss, r_rs.at[t, lane], up if lane < 2 else down, s)
+
+    def ring_step(t):
+        for lane in range(4):
+            drain(slots.at[t, lane], r_rs.at[t, lane])
+            slots[t, lane] = (slots[t, lane].astype(F32) + dwv[t + 1, lane].astype(F32)).astype(BF16)
+            if t < STEPS - 1:
+                remote(
+                    slots.at[t, lane], slots.at[t + 1, lane], r_ss, r_rs.at[t + 1, lane],
+                    up if lane < 2 else down, s,
+                )
+
+    pl.semaphore_wait(bar, 17)
+    spread(g_in, gbuf, q, send_q, g_ss, g_rs)
     for b in (1, 3, 2):
         qq = (q + b) % 4
-        remote(g_in, gbuf.at[rows(q)], g_ss, g_rs.at[q], dp, block(p, qq))
-        pp = (p + b) % 4
-        remote(w_in, wbuf.at[rows(p)], w_ss, w_rs.at[p], dp, block(pp, q))
         for f in range(4):
-            remote(
-                o_in.at[:, rows(block(f, qq))], abuf.at[rows(q), pl.ds(f * 128, 128)], a_ss, a_rs, dp, block(p, qq)
-            )
-
-    lg.wait()
-    lw.wait()
+            send_q(o_in.at[:, rows(block(f, qq))], abuf.at[rows(q), pl.ds(f * 128, 128)], a_ss, a_rs, qq)
+    pass_on(gbuf, q, send_q, g_ss, g_rs)
+    spread(w_in, wbuf, p, send_p, w_ss, w_rs)
+
     for cp in la:
         cp.wait()
-    for b in (1, 3, 2):
-        qq = (q + b) % 4
-        drain(gbuf.at[rows(qq)], g_rs.at[qq])
-        pp = (p + b) % 4
-        drain(wbuf.at[rows(pp)], w_rs.at[pp])
     drain(abuf.at[pl.ds(0, 384)], a_rs)
-
-    for a in range(4):
-        for b in range(4):
-            if a or b:
-                d = block((p + a) % 4, (q + b) % 4)
-                for t, (src, dst) in enumerate(((q_in, qh), (k_in, kh), (v_in, vh))):
-                    remote(src.at[:, rows(d)], dst.at[rows(s)], h_ss.at[t], h_rs.at[t], dp, d)
+    atbuf[...] = abuf[...].T
+    lg.wait()
+    arrive(gbuf, q, g_rs)
+
+    def project(n):
+        for half, chunk in ((0, (z + 7 - n) % 8), (1, (z + 1 + n) % 8)):
+            part = lax.dot_general(
+                atbuf[pl.ds(half * 256, 256), :], gbuf[:, rows(chunk, 512)], NN, preferred_element_type=F32
+            ).astype(BF16)
+            dwv[n, half * 2] = part[:128]
+            dwv[n, half * 2 + 1] = part[128:]
+
+    project(0)
+    ring_send(0)
+    pl.loop(1, 8)(project)
+    pass_on(wbuf, p, send_p, w_ss, w_rs)
+    send_heads(0)
+    ring_step(0)
+    lw.wait()
+    arrive(wbuf, p, w_rs)
+    send_heads(1)
+    send_heads(2)
 
     ones = jnp.ones((8, 128), F32)
     for n in range(2):
@@ -134,20 +204,15 @@
     for a in (1, 3, 2):
         pp = (p + a) % 4
         for b in range(4):
-            remote(gsnd.at[pp, pl.ds(b * 128, 128)], gh.at[rows(block(p, b))], ga_ss, ga_rs, dp, block(pp, q))
-            remote(rdsnd.at[pp, b], rdh.at[block(p, b)], rd_ss, rd_rs, dp, block(pp, q))
-
-    atbuf[...] = abuf[...].T
-
-    @pl.loop(0, 8)
-    def _(n):
-        cols = rows(n, 512)
-        dwv[:, cols] = lax.dot_general(
-            atbuf[...], gbuf[:, cols], NN, preferred_element_type=F32
-        ).astype(BF16)
-
-    cdw = pltpu.make_async_copy(dwv, dwp, dw_sem)
-    cdw.start()
+            send_p(gsnd.at[pp, pl.ds(b * 128, 128)], gh.at[rows(block(p, b))], ga_ss, ga_rs, pp)
+            send_p(rdsnd.at[pp, b], rdh.at[block(p, b)], rd_ss, rd_rs, pp)
+
+    lown = pltpu.make_async_copy(dwv.at[pl.ds(STEPS + 1, 7 - STEPS)], own, loc.at[17])
+    lown.start()
+    for t in range(1, STEPS):
+        ring_step(t)
+    lcur = pltpu.make_async_copy(slots.at[STEPS - 1], cur, loc.at[18])
+    lcur.start()
 
     for cp in lga:
         cp.wait()
@@ -155,15 +220,17 @@
         cp.wait()
     drain(gsnd.at[pl.ds(0, 3)], ga_rs)
     drain(rdsnd.at[pl.ds(0, 3)], rd_rs)
-    for t, dst in enumerate((qh, kh, vh)):
+    for t, (src, dst) in enumerate(heads):
         drain(dst.at[pl.ds(0, 1920)], h_rs.at[t])
-    cdw.wait()
+    lown.wait()
+    lcur.wait()
     drain(gbuf.at[pl.ds(0, 384)], g_ss)
     drain(wbuf.at[pl.ds(0, 384)], w_ss)
     drain(abuf.at[pl.ds(0, 384)], a_ss)
     drain(gsnd.at[pl.ds(0, 3)], ga_ss)
     drain(rdsnd.at[pl.ds(0, 3)], rd_ss)
-    for t, dst in enumerate((qh, kh, vh)):
+    drain(slots.at[pl.ds(0, STEPS)], r_ss)
+    for t, (src, dst) in enumerate(heads):
         drain(dst.at[pl.ds(0, 1920)], h_ss.at[t])
 
 
@@ -174,15 +241,16 @@
     return pl.pallas_call(
         gather_kernel,
         out_shape=(head, head, head, head, jax.ShapeDtypeStruct((16, 8, 128), F32),
-                   jax.ShapeDtypeStruct((512, 4096), BF16)),
+                   jax.ShapeDtypeStruct((4, 128, 512), BF16),
+                   jax.ShapeDtypeStruct((7 - STEPS, 4, 128, 512), BF16)),
         in_specs=[any_] * 6,
-        out_specs=(any_,) * 6,
+        out_specs=(any_,) * 7,
         scratch_shapes=[
             pltpu.VMEM((512, 4096), BF16), pltpu.VMEM((512, 4096), BF16), pltpu.VMEM((512, 512), BF16),
             pltpu.VMEM((512, 512), BF16), pltpu.VMEM((4, 512, 128), BF16), pltpu.VMEM((4, 4, 8, 128), F32),
-            pltpu.VMEM((512, 4096), BF16),
-            dma((4,)), dma((4,)), dma, dma((3,)), dma, dma,
-            dma, dma, dma, dma((3,)), dma, dma, dma((17,)), dma,
+            pltpu.VMEM((8, 4, 128, 512), BF16), pltpu.VMEM((STEPS, 4, 128, 512), BF16),
+            dma((6,)), dma((6,)), dma, dma((3,)), dma, dma, dma((STEPS, 4)),
+            dma, dma, dma, dma((3,)), dma, dma, dma, dma((19,)),
         ],
         compiler_params=pltpu.CompilerParams(collective_id=0, has_side_effects=True, vmem_limit_bytes=VMEM_LIMIT),
         name="gather_project",
@@ -260,9 +328,13 @@
 
 
 def return_kernel(
-    dq, dk, dv, dwp, oq, ok, ov, ow, pbuf, psum, zbuf, h_rs, p_rs, z_rs, h_ss, p_ss, z_ss, loc,
+    dq, dk, dv, cur, own_in, oq, ok, ov, ow,
+    own, slots, pbuf, csnd, cbuf, h_rs, r_rs, p_rs, c_rs, h_ss, r_ss, p_ss, c_ss, loc,
 ):
     dp, c, s, p, q, block = place()
+    z = dp // 2
+    up, down = ((z + 1) % 8) * 2 + c, ((z + 7) % 8) * 2 + c
+    mate = z * 2 + 1 - c
     bar = pltpu.get_barrier_semaphore()
     for a in range(4):
         for b in range(4):
@@ -270,76 +342,103 @@
                 pl.semaphore_signal(
                     bar, 1, device_id=(dp, block((p + a) % 4, (q + b) % 4)), device_id_type=MESH
                 )
-    for a in range(1, 16):
-        pl.semaphore_signal(bar, 1, device_id=((dp + a) % 16, s), device_id_type=MESH)
-    lp = pltpu.make_async_copy(dwp.at[rows(p)], pbuf.at[p], loc.at[0])
-    lp.start()
+    for d in (up, down, mate):
+        pl.semaphore_signal(bar, 1, device_id=(d, s), device_id_type=MESH)
+    lo = pltpu.make_async_copy(own_in, own, loc.at[0])
+    lo.start()
+    heads = ((dq, oq), (dk, ok), (dv, ov))
     lh = []
-    for t, (src, dst) in enumerate(((dq, oq), (dk, ok), (dv, ov))):
+    for t, (src, dst) in enumerate(heads):
         cp = pltpu.make_async_copy(src.at[rows(s)], dst.at[:, rows(s)], loc.at[1 + t])
         cp.start()
         lh.append(cp)
-    pl.semaphore_wait(bar, 30)
-    for a in (1, 3, 2):
-        pp = (p + a) % 4
-        remote(dwp.at[rows(pp)], pbuf.at[p], p_ss, p_rs, dp, block(pp, q))
-    lp.wait()
-    drain(pbuf.at[pl.ds(0, 3)], p_rs)
+    pl.semaphore_wait(bar, 18)
+    left = 7 - STEPS
+    for lane in range(4):
+        remote(cur.at[lane], slots.at[0, lane], r_ss, r_rs.at[0, lane], up if lane < 2 else down, s)
     for a in range(4):
         for b in range(4):
             if a or b:
                 d = block((p + a) % 4, (q + b) % 4)
-                for t, (src, dst) in enumerate(((dq, oq), (dk, ok), (dv, ov))):
+                for t, (src, dst) in enumerate(heads):
                     remote(src.at[rows(d)], dst.at[:, rows(s)], h_ss.at[t], h_rs.at[t], dp, d)
-    for n in range(16):
-        cs = slice(n * 256, (n + 1) * 256)
-        tot = pbuf[0, :, cs].astype(F32)
-        for a in range(1, 4):
-            tot += pbuf[a, :, cs].astype(F32)
-        psum[n] = tot.astype(BF16)
-    lz = pltpu.make_async_copy(psum.at[dp], zbuf.at[dp], loc.at[4])
-    lz.start()
-    for a in range(1, 16):
-        d = (dp + a) % 16
-        remote(psum.at[d], zbuf.at[dp], z_ss, z_rs, d, s)
-    lz.wait()
-    drain(zbuf.at[pl.ds(0, 15)], z_rs)
-    tot = zbuf[0].astype(F32)
-    for n in range(1, 16):
-        tot += zbuf[n].astype(F32)
-    ow[...] = tot
+    lo.wait()
+    for t in range(left):
+        for lane in range(4):
+            drain(slots.at[t, lane], r_rs.at[t, lane])
+            slots[t, lane] = (slots[t, lane].astype(F32) + own[t, lane].astype(F32)).astype(BF16)
+            if t < left - 1:
+                remote(
+                    slots.at[t, lane], slots.at[t + 1, lane], r_ss, r_rs.at[t + 1, lane],
+                    up if lane < 2 else down, s,
+                )
+    lp = pltpu.make_async_copy(slots.at[left - 1, p], pbuf.at[p], loc.at[4])
+    lp.start()
+    for a in (1, 3, 2):
+        pp = (p + a) % 4
+        remote(slots.at[left - 1, pp], pbuf.at[p], p_ss, p_rs, dp, block(pp, q))
+    lp.wait()
+    drain(pbuf.at[pl.ds(0, 3)], p_rs)
+    tot = pbuf[0].astype(F32)
+    for a in range(1, 4):
+        tot += pbuf[a].astype(F32)
+    csnd[0] = tot[:, :256]
+    csnd[1] = tot[:, 256:]
+    remote(csnd.at[1 - c], cbuf, c_ss, c_rs, mate, s)
+    drain(cbuf, c_rs)
+    ow[...] = csnd[c] + cbuf[...]
     for cp in lh:
         cp.wait()
-    for t, src in enumerate((dq, dk, dv)):
+    for t, (src, dst) in enumerate(heads):
         drain(src.at[pl.ds(0, 1920)], h_rs.at[t])
+    drain(slots, r_ss)
     drain(pbuf.at[pl.ds(0, 3)], p_ss)
-    drain(zbuf.at[pl.ds(0, 15)], z_ss)
-    for t, src in enumerate((dq, dk, dv)):
+    drain(cbuf, c_ss)
+    for t, (src, dst) in enumerate(heads):
         drain(src.at[pl.ds(0, 1920)], h_ss.at[t])
 
 
-def give_back(dq, dk, dv, dwp):
+def give_back(dq, dk, dv, cur, own):
     any_ = pl.BlockSpec(memory_space=pl.ANY)
     tok = jax.ShapeDtypeStruct((128, 2048), BF16)
     dma = pltpu.SemaphoreType.DMA
+    left = 7 - STEPS
     return pl.pallas_call(
         return_kernel,
         out_shape=(tok, tok, tok, jax.ShapeDtypeStruct((128, 256), F32)),
-        in_specs=[any_] * 4,
+        in_specs=[any_] * 5,
         out_specs=(any_, any_, any_, pl.BlockSpec(memory_space=pltpu.VMEM)),
         scratch_shapes=[
-            pltpu.VMEM((4, 128, 4096), BF16), pltpu.VMEM((16, 128, 256), BF16), pltpu.VMEM((16, 128, 256), BF16),
-            dma((3,)), dma, dma, dma((3,)), dma, dma, dma((5,)),
+            pltpu.VMEM((left, 4, 128, 512), BF16), pltpu.VMEM((left, 4, 128, 512), BF16),
+            pltpu.VMEM((4, 128, 512), BF16), pltpu.VMEM((2, 128, 256), F32), pltpu.VMEM((128, 256), F32),
+            dma((3,)), dma((left, 4)), dma, dma, dma((3,)), dma, dma, dma, dma((5,)),
         ],
         compiler_params=pltpu.CompilerParams(collective_id=1, has_side_effects=True, vmem_limit_bytes=VMEM_LIMIT),
         name="return_reduce",
-    )(dq, dk, dv, dwp)
+    )(dq, dk, dv, cur, own)
+
+
+def finish_kernel(*refs):
+    n = len(refs) // 2
+    for i in range(n):
+        refs[n + i][...] = refs[i][...]
+
+
+def finish(*arrays):
+    vm = pl.BlockSpec(memory_space=pltpu.VMEM)
+    return pl.pallas_call(
+        finish_kernel,
+        out_shape=tuple(jax.ShapeDtypeStruct(a.shape, a.dtype) for a in arrays),
+        in_specs=[vm] * len(arrays),
+        out_specs=(vm,) * len(arrays),
+        name="finish",
+    )(*arrays)
 
 
 def shards(queries, keys, values, attn, grad_out, w_out, starts):
-    qh, kh, vh, gh, rdh, dwp = gather(queries, keys, values, attn, grad_out, w_out)
+    qh, kh, vh, gh, rdh, cur, own = gather(queries, keys, values, attn, grad_out, w_out)
     dq, dk, dv = attention(starts, qh, kh, vh, gh, rdh)
-    return give_back(dq, dk, dv, dwp)
+    return finish(*give_back(dq, dk, dv, cur, own))
 
 
 def solution(mesh):

time: 162 us -> 131 us (0.81)
  Pallas kernels: 154 us -> 130 us
  local copies, waits for them, and re-layouts: 7.21 us -> 0 us
    pallas_call x1, Pallas kernels: 60.5 us -> 34.2 us  [give_back(): pl.pallas_call(return_kernel, out_shape=(tok, tok, tok, jax.ShapeDtypeStr...]
    unnamed x4 -> x0, local copies, waits for them, and re-layouts: 7.21 us -> none
    pallas_call x0 -> x1, Pallas kernels: none -> 2.59 us  [finish(): pl.pallas_call(finish_kernel, out_shape=tuple((jax.ShapeDtypeStruct(a.sha...]
where the time goes in v2:
time: 131 us; the launch traced here: 130 us
  Pallas kernels  130 us (99%)
    pallas_call x1, Pallas kernels, gather(): pl.pallas_call(gather_kernel, out_shape=(head, head, head, head, jax.Shap...  80.9 us
    pallas_call x1, Pallas kernels, give_back(): pl.pallas_call(return_kernel, out_shape=(tok, tok, tok, jax.ShapeDtypeStr...  34.2 us
    pallas_call x1, Pallas kernels, attention(): pl.pallas_call(attn_kernel, out_shape=(head, head, head), in_specs=[pl.Bl...  12.1 us

profile of v2, /device:TPU:1, one launch (start us, length us, event | category | flops | bytes accessed | tf_op | source)
XLA Modules:
  0.0 130.5 jit_solution(9153263172477649144)
XLA Ops:
  0.6 80.9 %gather_project.1 = (bf16[2048,128]{1,0:T(8,128)(2,1)}, bf16[2048,128]{1,0:T(8,128)(2,1)}, bf16[2048,128]{1,0:T(8,128)(2,1)}, bf16[2048,128]{1,0:T(8,128)(2,1)},...) custom-call(bf16[128,2048]{1,0:T(8,128)(2,1)} %q_in.1, ...), custom_call_target="tpu_custom_call" | custom-call | tf_op jit(solution)/shard_map/gather_project/pallas_call | solution.py:241
  81.6 12.1 %attention_grads.1 = (bf16[2048,128]{1,0:T(8,128)(2,1)}, bf16[2048,128]{1,0:T(8,128)(2,1)}, bf16[2048,128]{1,0:T(8,128)(2,1)}) custom-call(s32[1,8]{1,0:T(1,128)} %first.1, bf16[2048,128]{1,0:T(8,128)(2,1)} %get-tuple-element.18.q, bf16[2048,128]{1,0:T(8,128)(2,1)} %get-tuple-element.19.k, bf16[2048,128]{1,0:T(8,128)(2,1)} %get-tuple-element.20.v, ...), custom_call_target="tpu_custom_call" | custom-call | tf_op jit(solution)/shard_map/attention_grads/pallas_call | solution.py:319
  93.7 34.2 %return_reduce.1 = (bf16[128,2048]{1,0:T(8,128)(2,1)}, bf16[128,2048]{1,0:T(8,128)(2,1)}, bf16[128,2048]{1,0:T(8,128)(2,1)}, f32[128,256]{1,0:T(8,128)}) custom-call(bf16[2048,128]{1,0:T(8,128)(2,1)} %get-tuple-element.23.dq, bf16[2048,128]{1,0:T(8,128)(2,1)} %get-tuple-element.24.dk, bf16[2048,128]{1,0:T(8,128)(2,1)} %get-tuple-element.25.dv, ...), custom_call_target="tpu_custom_call" | custom-call | tf_op jit(solution)/shard_map/return_reduce/pallas_call | solution.py:406
  127.9 2.6 %finish.1 = (bf16[128,2048]{1,0:T(8,128)(2,1)}, bf16[128,2048]{1,0:T(8,128)(2,1)}, bf16[128,2048]{1,0:T(8,128)(2,1)}, f32[128,256]{1,0:T(8,128)}) custom-call(bf16[128,2048]{1,0:T(8,128)(2,1)} %get-tuple-element.28.refs_0_, bf16[128,2048]{1,0:T(8,128)(2,1)} %get-tuple-element.29.refs_1_, bf16[128,2048]{1,0:T(8,128)(2,1)} %get-tuple-element.30.refs_2_, ...), custom_call_target="tpu_custom_call" | custom-call | tf_op jit(solution)/shard_map/finish/pallas_call | solution.py:429

commit v3 on v0

v3 whole, which is shorter than its diff:
```python
import functools

import jax
import jax.numpy as jnp
from jax import lax
from jax.experimental import pallas as pl
from jax.experimental.pallas import tpu as pltpu
from jax.sharding import PartitionSpec as P

HDIM = 128
MESH = pl.DeviceIdType.MESH
BF16 = jnp.bfloat16
F32 = jnp.float32
NT = (((1,), (1,)), ((), ()))
NN = (((1,), (0,)), ((), ()))
TN = (((0,), (0,)), ((), ()))
VMEM_LIMIT = 56 << 20


def place():
    dp = lax.axis_index("dp")
    s = lax.axis_index("seq")
    c = dp % 2
    x, y = s // 4, s % 4
    p = x * (1 - c) + y * c
    q = y * (1 - c) + x * c
    sp, sq = 4 - 3 * c, 1 + 3 * c

    def block(pp, qq):
        return pp * sp + qq * sq

    return dp, c, s, p, q, block


def remote(src, dst, ssem, rsem, dp, s):
    cp = pltpu.make_async_remote_copy(
        src_ref=src, dst_ref=dst, send_sem=ssem, recv_sem=rsem, device_id=(dp, s), device_id_type=MESH
    )
    cp.start()


def drain(ref, sem):
    pltpu.make_async_copy(ref, ref, sem).wait()


def rows(i, n=128):
    return pl.ds(pl.multiple_of(i * n, n), n)


BLK = 512
NBLK = 2048 // BLK
SCALE = HDIM ** (-0.5)
LOG2E = 1.4426950408889634


def spread(pieces, me, send_next, send_prev, ss, rs):
    for half, send, sem in ((0, send_next, 0), (1, send_prev, 1), (1, send_next, 2), (0, send_prev, 3)):
        for src, dst in pieces(me, half):
            send(src, dst, ss, rs.at[sem])


def pass_on(pieces, whole, me, send_next, send_prev, ss, rs):
    nxt, prv = (me + 1) % 4, (me + 3) % 4
    drain(whole, rs.at[0])
    for _, ref in pieces(prv, 0):
        send_next(ref, ref, ss, rs.at[4])
    drain(whole, rs.at[1])
    for _, ref in pieces(nxt, 1):
        send_prev(ref, ref, ss, rs.at[5])


def arrive(whole, rs):
    for sem in (2, 3, 4, 5):
        drain(whole, rs.at[sem])


def attend(i, first, q, k, v, g, rd, dq, sbuf, dka, dva):
    qs = pl.ds(i * BLK, BLK)
    pos = lax.broadcasted_iota(jnp.int32, (1, BLK), 1) + i * BLK
    seg = jnp.zeros((1, BLK), jnp.int32)
    for e in range(8):
        st = first[0, e]
        seg = jnp.where(pos >= st, jnp.maximum(seg, st), seg)
    rdi = jnp.concatenate([rd[i * (BLK // 128) + t][:1] for t in range(BLK // 128)], axis=1)

    def scores(j, m):
        ks = pl.ds(pl.multiple_of(j * BLK, BLK), BLK)
        sc = lax.dot_general(k[ks, :], q[qs, :], NT, preferred_element_type=F32) * (SCALE * LOG2E)
        kp = lax.broadcasted_iota(jnp.int32, (BLK, BLK), 0) + j * BLK
        sc = jnp.where((kp <= pos) & (kp >= seg), sc, -1e30)
        sbuf[ks, :] = sc
        return jnp.maximum(m, jnp.max(sc.reshape(BLK // 8, 8, BLK), axis=0))

    m = lax.fori_loop(0, i + 1, scores, jnp.full((8, BLK), -1e30, F32))
    m = jnp.max(m, axis=0, keepdims=True)

    def expo(j, tot):
        ks = pl.ds(pl.multiple_of(j * BLK, BLK), BLK)
        e = jnp.exp2(sbuf[ks, :] - m)
        sbuf[ks, :] = e
        return tot + jnp.sum(e.reshape(BLK // 8, 8, BLK), axis=0)

    tot = lax.fori_loop(0, i + 1, expo, jnp.zeros((8, BLK), F32))
    inv = 1.0 / jnp.sum(tot, axis=0, keepdims=True)

    def grads(j, acc):
        ks = pl.ds(pl.multiple_of(j * BLK, BLK), BLK)
        prob = sbuf[ks, :] * inv
        gp = lax.dot_general(v[ks, :], g[qs, :], NT, preferred_element_type=F32)
        ds = (prob * (gp - rdi)).astype(BF16)
        dva[ks, :] += lax.dot_general(prob.astype(BF16), g[qs, :], NN, preferred_element_type=F32)
        dka[ks, :] += lax.dot_general(ds, q[qs, :], NN, preferred_element_type=F32)
        return acc + lax.dot_general(ds, k[ks, :], TN, preferred_element_type=F32)

    acc = lax.fori_loop(0, i + 1, grads, jnp.zeros((BLK, HDIM), F32))
    dq[qs, :] = (acc * SCALE).astype(BF16)


def whole_kernel(
    q_in, k_in, v_in, o_in, g_in, w_in, first,
    oq, ok, ov, ow,
    gbuf, wbuf, abuf, atbuf, gsnd, rdsnd, dwv, slots, qh, kh, vh, gh, rdh,
    sbuf, dka, dva, dq, dk, dv, pbuf, csnd, cbuf,
    g_rs, wx_rs, wz_rs, a_rs, h_rs, ga_rs, rd_rs, r_rs, b_rs, p_rs, c_rs,
    g_ss, wx_ss, wz_ss, a_ss, h_ss, ga_ss, rd_ss, r_ss, b_ss, p_ss, c_ss,
    loc, ga_loc, rd_loc, b_loc,
):
    dp, c, s, p, q, block = place()
    z = dp // 2
    zq = z % 4
    up, down = ((z + 1) % 8) * 2 + c, ((z + 7) % 8) * 2 + c
    mate = z * 2 + 1 - c
    bar = pltpu.get_barrier_semaphore()
    for a in range(4):
        for b in range(4):
            if a or b:
                pl.semaphore_signal(
                    bar, 1, device_id=(dp, block((p + a) % 4, (q + b) % 4)), device_id_type=MESH
                )
    for d in (up, down, mate):
        pl.semaphore_signal(bar, 1, device_id=(d, s), device_id_type=MESH)

    lg = pltpu.make_async_copy(g_in, gbuf.at[rows(q)], loc.at[0])
    lw = pltpu.make_async_copy(w_in, wbuf.at[rows(p)], loc.at[1])
    lg.start()
    lw.start()
    la = []
    for pp in range(4):
        cp = pltpu.make_async_copy(
            o_in.at[:, rows(block(pp, q))], abuf.at[rows(q), pl.ds(pp * 128, 128)], loc.at[2 + pp]
        )
        cp.start()
        la.append(cp)
    heads = ((q_in, qh), (k_in, kh), (v_in, vh))
    lh = []
    for t, (src, dst) in enumerate(heads):
        cp = pltpu.make_async_copy(src.at[:, rows(s)], dst.at[rows(s)], loc.at[6 + t])
        cp.start()
        lh.append(cp)

    def to_next(src, dst, ssem, rsem):
        remote(src, dst, ssem, rsem, dp, block(p, (q + 1) % 4))

    def to_prev(src, dst, ssem, rsem):
        remote(src, dst, ssem, rsem, dp, block(p, (q + 3) % 4))

    def to_up(src, dst, ssem, rsem):
        remote(src, dst, ssem, rsem, up, s)

    def to_down(src, dst, ssem, rsem):
        remote(src, dst, ssem, rsem, down, s)

    def g_pieces(who, half):
        ref = gbuf.at[rows(who * 2 + half, 64)]
        return [(g_in.at[pl.ds(half * 64, 64)], ref)]

    def w_pieces(who, half):
        refs = [wbuf.at[rows(((p + a) % 4) * 8 + who * 2 + half, 16)] for a in range(1, 4)]
        return [(ref, ref) for ref in refs]

    g_half, w_half = gbuf.at[pl.ds(0, 64)], wbuf.at[pl.ds(0, 48)]

    def send_heads(t):
        src, dst = heads[t]
        for a in range(4):
            for b in range(4):
                if a or b:
                    d = block((p + a) % 4, (q + b) % 4)
                    remote(src.at[:, rows(d)], dst.at[rows(s)], h_ss.at[t], h_rs.at[t], dp, d)

    def ring_send():
        for lane in range(4):
            remote(dwv.at[0, lane], slots.at[0, lane], r_ss, r_rs.at[0, lane], up if lane < 2 else down, s)

    def ring_step(t):
        for lane in (0, 2, 1, 3):
            drain(slots.at[t, lane], r_rs.at[t, lane])
            slots[t, lane] = (slots[t, lane].astype(F32) + dwv[t + 1, lane].astype(F32)).astype(BF16)
            if t < 6:
                remote(
                    slots.at[t, lane], slots.at[t + 1, lane], r_ss, r_rs.at[t + 1, lane],
                    up if lane < 2 else down, s,
                )

    def project(n):
        for half, chunk in ((0, (z + 7 - n) % 8), (1, (z + 1 + n) % 8)):
            part = lax.dot_general(
                atbuf[pl.ds(half * 256, 256), :], gbuf[:, rows(chunk, 512)], NN, preferred_element_type=F32
            ).astype(BF16)
            dwv[n, half * 2] = part[:128]
            dwv[n, half * 2 + 1] = part[128:]

    pl.semaphore_wait(bar, 18)
    for a in (1, 3, 2):
        pp = (p + a) % 4
        remote(
            w_in.at[rows(zq, 32)], wbuf.at[rows(p * 4 + zq, 32)], wx_ss, wx_rs.at[p], dp, block(pp, q)
        )
    spread(g_pieces, q, to_next, to_prev, g_ss, g_rs)
    for b in (1, 3, 2):
        qq = (q + b) % 4
        for f in range(4):
            remote(
                o_in.at[:, rows(block(f, qq))], abuf.at[rows(q), pl.ds(f * 128, 128)], a_ss, a_rs, dp, block(p, qq)
            )
    for a in (1, 3, 2):
        pp = (p + a) % 4
        drain(wbuf.at[rows(pp * 4 + zq, 32)], wx_rs.at[pp])
    spread(w_pieces, zq, to_up, to_down, wz_ss, wz_rs)
    pass_on(g_pieces, g_half, q, to_next, to_prev, g_ss, g_rs)
    send_heads(0)
    for cp in la:
        cp.wait()
    drain(abuf.at[pl.ds(0, 384)], a_rs)
    atbuf[...] = abuf[...].T
    pass_on(w_pieces, w_half, zq, to_up, to_down, wz_ss, wz_rs)
    lg.wait()
    arrive(g_half, g_rs)
    send_heads(1)
    send_heads(2)
    pl.loop(0, 8)(project)
    lw.wait()
    arrive(w_half, wz_rs)
    ring_send()

    for n in range(2):
        ga = lax.dot_general(
            gbuf[...], wbuf[pl.ds(n * 256, 256), :], NT, preferred_element_type=F32
        ).astype(BF16)
        for m in range(2):
            f = n * 2 + m
            gf = ga[:, m * 128 : (m + 1) * 128]
            gsnd[f] = gf
            prod = gf.astype(F32) * abuf[:, f * 128 : (f + 1) * 128].astype(F32)
            rd = jnp.sum(prod.T, axis=0, keepdims=True)
            for t in range(4):
                rdsnd[f, t] = jnp.broadcast_to(rd[:, t * 128 : (t + 1) * 128], (8, 128))

            @pl.when(p == f)
            def _():
                for b in range(4):
                    pltpu.make_async_copy(gsnd.at[f, pl.ds(b * 128, 128)], gh.at[rows(block(p, b))], ga_loc).start()
                    pltpu.make_async_copy(rdsnd.at[f, b], rdh.at[block(p, b)], rd_loc).start()

            @pl.when(p != f)
            def _():
                for b in range(4):
                    remote(
                        gsnd.at[f, pl.ds(b * 128, 128)], gh.at[rows(block(p, b))], ga_ss, ga_rs, dp, block(f, q)
                    )
                    remote(rdsnd.at[f, b], rdh.at[block(p, b)], rd_ss, rd_rs, dp, block(f, q))

    ring_step(0)
    dka[...] = jnp.zeros_like(dka)
    dva[...] = jnp.zeros_like(dva)
    for cp in lh:
        cp.wait()
    drain(gsnd.at[0], ga_loc)
    drain(rdsnd.at[0], rd_loc)
    for t, (src, dst) in enumerate(heads):
        drain(dst.at[pl.ds(0, 1920)], h_rs.at[t])
    drain(gsnd.at[pl.ds(0, 3)], ga_rs)
    drain(rdsnd.at[pl.ds(0, 3)], rd_rs)
    ring_step(1)

    back = ((dq, oq), (dk, ok), (dv, ov))
    for i in range(NBLK - 1, -1, -1):
        attend(i, first, qh, kh, vh, gh, rdh, dq, sbuf, dka, dva)
        qs = pl.ds(i * BLK, BLK)
        dk[qs, :] = (dka[qs, :] * SCALE).astype(BF16)
        dv[qs, :] = dva[qs, :].astype(BF16)
        for t in range(4):
            d = i * 4 + (s + t) % 4

            @pl.when(d == s)
            def _():
                for n, (src, dst) in enumerate(back):
                    pltpu.make_async_copy(src.at[rows(d)], dst.at[:, rows(s)], b_loc.at[n]).start()

            @pl.when(d != s)
            def _():
                for n, (src, dst) in enumerate(back):
                    remote(src.at[rows(d)], dst.at[:, rows(s)], b_ss.at[n], b_rs.at[n], dp, d)
        if i in (3, 2, 0):
            ring_step({3: 2, 2: 3, 0: 4}[i])
    ring_step(5)
    ring_step(6)

    lp = pltpu.make_async_copy(slots.at[6, p], pbuf.at[p], loc.at[9])
    lp.start()
    for a in (1, 3, 2):
        pp = (p + a) % 4
        remote(slots.at[6, pp], pbuf.at[p], p_ss, p_rs, dp, block(pp, q))
    lp.wait()
    drain(pbuf.at[pl.ds(0, 3)], p_rs)
    tot = pbuf[0].astype(F32)
    for a in range(1, 4):
        tot += pbuf[a].astype(F32)
    csnd[0] = tot[:, :256]
    csnd[1] = tot[:, 256:]
    remote(csnd.at[1 - c], cbuf, c_ss, c_rs, mate, s)
    drain(cbuf, c_rs)
    ow[...] = csnd[c] + cbuf[...]

    for n, (src, dst) in enumerate(back):
        drain(src.at[pl.ds(0, 128)], b_loc.at[n])
        drain(src.at[pl.ds(0, 1920)], b_rs.at[n])
        drain(src.at[pl.ds(0, 1920)], b_ss.at[n])
    drain(gbuf.at[pl.ds(0, 384)], g_ss)
    drain(wbuf.at[pl.ds(0, 96)], wx_ss)
    drain(wbuf.at[pl.ds(0, 288)], wz_ss)
    drain(abuf.at[pl.ds(0, 384)], a_ss)
    drain(gsnd.at[pl.ds(0, 3)], ga_ss)
    drain(rdsnd.at[pl.ds(0, 3)], rd_ss)
    drain(slots, r_ss)
    drain(pbuf.at[pl.ds(0, 3)], p_ss)
    drain(cbuf, c_ss)
    for t, (src, dst) in enumerate(heads):
        drain(dst.at[pl.ds(0, 1920)], h_ss.at[t])


def run_whole(queries, keys, values, attn, grad_out, w_out, starts):
    any_ = pl.BlockSpec(memory_space=pl.ANY)
    tok = jax.ShapeDtypeStruct((128, 2048), BF16)
    dma = pltpu.SemaphoreType.DMA
    head = pltpu.VMEM((2048, HDIM), BF16)
    acc = pltpu.VMEM((2048, HDIM), F32)
    return pl.pallas_call(
        whole_kernel,
        out_shape=(tok, tok, tok, jax.ShapeDtypeStruct((128, 256), F32)),
        in_specs=[any_] * 6 + [pl.BlockSpec(memory_space=pltpu.SMEM)],
        out_specs=(any_, any_, any_, pl.BlockSpec(memory_space=pltpu.VMEM)),
        scratch_shapes=[
            pltpu.VMEM((512, 4096), BF16), pltpu.VMEM((512, 4096), BF16), pltpu.VMEM((512, 512), BF16),
            pltpu.VMEM((512, 512), BF16), pltpu.VMEM((4, 512, 128), BF16), pltpu.VMEM((4, 4, 8, 128), F32),
            pltpu.VMEM((8, 4, 128, 512), BF16), pltpu.VMEM((7, 4, 128, 512), BF16),
            head, head, head, head, pltpu.VMEM((16, 8, 128), F32),
            pltpu.VMEM((2048, BLK), F32), acc, acc, head, head, head,
            pltpu.VMEM((4, 128, 512), BF16), pltpu.VMEM((2, 128, 256), F32), pltpu.VMEM((128, 256), F32),
            dma((6,)), dma((4,)), dma((6,)), dma, dma((3,)), dma, dma, dma((7, 4)), dma((3,)), dma, dma,
            dma, dma, dma, dma, dma((3,)), dma, dma, dma, dma((3,)), dma, dma,
            dma((10,)), dma, dma, dma((3,)),
        ],
        compiler_params=pltpu.CompilerParams(collective_id=0, has_side_effects=True, vmem_limit_bytes=VMEM_LIMIT),
        name="whole",
    )(queries, keys, values, attn, grad_out, w_out, starts)


def finish_kernel(*refs):
    n = len(refs) // 2
    for i in range(n):
        refs[n + i][...] = refs[i][...]


def finish(*arrays):
    vm = pl.BlockSpec(memory_space=pltpu.VMEM)
    return pl.pallas_call(
        finish_kernel,
        out_shape=tuple(jax.ShapeDtypeStruct(a.shape, a.dtype) for a in arrays),
        in_specs=[vm] * len(arrays),
        out_specs=(vm,) * len(arrays),
        name="finish",
    )(*arrays)


def shards(queries, keys, values, attn, grad_out, w_out, starts):
    return finish(*run_whole(queries, keys, values, attn, grad_out, w_out, starts))


def solution(mesh):
    tok = P(("dp", "seq"), None)
    return jax.shard_map(
        shards,
        mesh=mesh,
        in_specs=(tok, tok, tok, tok, tok, P("seq", None), P("dp", None)),
        out_specs=(tok, tok, tok, P("seq", "dp")),
        check_vma=False,
    )
```

time: 271 us -> 107 us (0.39); the launches traced: 267 us -> 107 us
  waiting for transfers between devices: 119 us -> 0 us
  Pallas kernels: 0 us -> 106 us
  matrix products: 45.2 us -> 0 us
  starting transfers between devices: 33.8 us -> 0 us
  local copies, waits for them, and re-layouts: 27 us -> 0 us
  other arithmetic: 24.7 us -> 0 us
  between operations: 14.2 us -> 0.64 us
    pallas_call x0 -> x2, Pallas kernels: none -> 106 us  [the longest x1 104 us: run_whole(): pl.pallas_call(whole_kernel, out_shape=(tok, tok, tok, jax.ShapeDtypeStru...]
    all_gather x1 -> x0, waiting for transfers between devices: 62.3 us -> none  [shards(): full_grad = lax.all_gather(grad_out, 'seq', axis=0, tiled=True)]
    all_to_all x7 -> x0, waiting for transfers between devices: 56.2 us -> none  [the longest x1 12.8 us: shards(): lax.all_to_all(keys, 'seq', split_axis=1, concat_axis=0, tiled=True)]
    dot_general x22 -> x0, matrix products: 45.2 us -> none  [the longest x4 10.2 us: tile_scores(): jnp.einsum('qhd,khd->hqk', q_blk, key_tile, preferred_element_type=jnp.fl...]
    all_to_all x7 -> x0, starting transfers between devices: 33.7 us -> none  [the longest x1 7.58 us: shards(): lax.all_to_all(queries, 'seq', split_axis=1, concat_axis=0, tiled=True)]
    reduce_sum x8 -> x0, other arithmetic: 12.2 us -> none  [the longest x4 7.76 us: step(): jnp.sum(jnp.where(live, jnp.exp(scores - top), 0.0), axis=-1, keepdims=True)]
    all_to_all x7 -> x0, local copies, waits for them, and re-layouts: 10.4 us -> none  [the longest x1 2.2 us: shards(): lax.all_to_all(queries, 'seq', split_axis=1, concat_axis=0, tiled=True)]
    unnamed x21 -> x0, local copies, waits for them, and re-layouts: 9.17 us -> none
  transfers between devices with their start and end apart: 9 -> 0, of which waited for: 8 -> 0; matrix products, arithmetic and copies ran while one was open for 32% -> 0% of each run, Pallas kernels for 0% -> 0%
where the time goes in v3:
time: 107 us
  Pallas kernels  106 us (99%)
    pallas_call x1, Pallas kernels, run_whole(): pl.pallas_call(whole_kernel, out_shape=(tok, tok, tok, jax.ShapeDtypeStru...  104 us
    pallas_call x1, Pallas kernels, finish(): pl.pallas_call(finish_kernel, out_shape=tuple((jax.ShapeDtypeStruct(a.sha...  2.59 us

profile of v3, /device:TPU:1, one launch (start us, length us, event | category | flops | bytes accessed | tf_op | source)
XLA Modules:
  0.0 106.8 jit_solution(6232945785028193255)
XLA Ops:
  0.6 103.6 %whole.1 = (bf16[128,2048]{1,0:T(8,128)(2,1)}, bf16[128,2048]{1,0:T(8,128)(2,1)}, bf16[128,2048]{1,0:T(8,128)(2,1)}, f32[128,256]{1,0:T(8,128)}) custom-call(bf16[128,2048]{1,0:T(8,128)(2,1)} %q_in.1, bf16[128,2048]{1,0:T(8,128)(2,1)} %k_in.1, bf16[128,2048]{1,0:T(8,128)(2,1)} %v_in.1, bf16[128,2048]{1,0:T(8,128)(2,1)} %o_in.1, bf16[128,4096]{1,0:T(8,128)(2,1)} %g_in.1, ...), custom_call_target="tpu_custom_call" | custom-call | tf_op jit(solution)/shard_map/whole/pallas_call | solution.py:348
  104.2 2.6 %finish.1 = (bf16[128,2048]{1,0:T(8,128)(2,1)}, bf16[128,2048]{1,0:T(8,128)(2,1)}, bf16[128,2048]{1,0:T(8,128)(2,1)}, f32[128,256]{1,0:T(8,128)}) custom-call(bf16[128,2048]{1,0:T(8,128)(2,1)} %get-tuple-element.8.refs_0_, bf16[128,2048]{1,0:T(8,128)(2,1)} %get-tuple-element.9.refs_1_, bf16[128,2048]{1,0:T(8,128)(2,1)} %get-tuple-element.10.refs_2_, ...), custom_call_target="tpu_custom_call" | custom-call | tf_op jit(solution)/shard_map/finish/pallas_call | solution.py:377

commit v4 on v3

--- a/solution.py
+++ b/solution.py
@@ -51,6 +51,8 @@
 NBLK = 2048 // BLK
 SCALE = HDIM ** (-0.5)
 LOG2E = 1.4426950408889634
+FIRST_STEPS = 3
+LAST_STEPS = 2
 
 
 def spread(pieces, me, send_next, send_prev, ss, rs):
@@ -69,12 +71,12 @@
         send_prev(ref, ref, ss, rs.at[5])
 
 
-def arrive(whole, rs):
-    for sem in (2, 3, 4, 5):
+def arrive(whole, rs, sems=(2, 3, 4, 5)):
+    for sem in sems:
         drain(whole, rs.at[sem])
 
 
-def attend(i, first, q, k, v, g, rd, dq, sbuf, dka, dva):
+def attend(i, first, q, k, v, g, rd, dq, sbuf, dka, dva, between):
     qs = pl.ds(i * BLK, BLK)
     pos = lax.broadcasted_iota(jnp.int32, (1, BLK), 1) + i * BLK
     seg = jnp.zeros((1, BLK), jnp.int32)
@@ -84,27 +86,35 @@
     rdi = jnp.concatenate([rd[i * (BLK // 128) + t][:1] for t in range(BLK // 128)], axis=1)
 
     def scores(j, m):
-        ks = pl.ds(pl.multiple_of(j * BLK, BLK), BLK)
+        ks = pl.ds(j * BLK, BLK)
         sc = lax.dot_general(k[ks, :], q[qs, :], NT, preferred_element_type=F32) * (SCALE * LOG2E)
-        kp = lax.broadcasted_iota(jnp.int32, (BLK, BLK), 0) + j * BLK
-        sc = jnp.where((kp <= pos) & (kp >= seg), sc, -1e30)
+        kp = lax.broadcasted_iota(jnp.int32, (BLK, BLK), 0)
+        live = kp >= seg - j * BLK
+        if j == i:
+            live = live & (kp <= pos - j * BLK)
+        sc = jnp.where(live, sc, -1e30)
         sbuf[ks, :] = sc
         return jnp.maximum(m, jnp.max(sc.reshape(BLK // 8, 8, BLK), axis=0))
 
-    m = lax.fori_loop(0, i + 1, scores, jnp.full((8, BLK), -1e30, F32))
+    m = jnp.full((8, BLK), -1e30, F32)
+    for j in range(i + 1):
+        m = scores(j, m)
     m = jnp.max(m, axis=0, keepdims=True)
 
     def expo(j, tot):
-        ks = pl.ds(pl.multiple_of(j * BLK, BLK), BLK)
+        ks = pl.ds(j * BLK, BLK)
         e = jnp.exp2(sbuf[ks, :] - m)
         sbuf[ks, :] = e
         return tot + jnp.sum(e.reshape(BLK // 8, 8, BLK), axis=0)
 
-    tot = lax.fori_loop(0, i + 1, expo, jnp.zeros((8, BLK), F32))
+    tot = jnp.zeros((8, BLK), F32)
+    for j in range(i + 1):
+        tot = expo(j, tot)
     inv = 1.0 / jnp.sum(tot, axis=0, keepdims=True)
+    between()
 
     def grads(j, acc):
-        ks = pl.ds(pl.multiple_of(j * BLK, BLK), BLK)
+        ks = pl.ds(j * BLK, BLK)
         prob = sbuf[ks, :] * inv
         gp = lax.dot_general(v[ks, :], g[qs, :], NT, preferred_element_type=F32)
         ds = (prob * (gp - rdi)).astype(BF16)
@@ -112,18 +122,20 @@
         dka[ks, :] += lax.dot_general(ds, q[qs, :], NN, preferred_element_type=F32)
         return acc + lax.dot_general(ds, k[ks, :], TN, preferred_element_type=F32)
 
-    acc = lax.fori_loop(0, i + 1, grads, jnp.zeros((BLK, HDIM), F32))
+    acc = jnp.zeros((BLK, HDIM), F32)
+    for j in range(i + 1):
+        acc = grads(j, acc)
     dq[qs, :] = (acc * SCALE).astype(BF16)
 
 
 def whole_kernel(
     q_in, k_in, v_in, o_in, g_in, w_in, first,
     oq, ok, ov, ow,
-    gbuf, wbuf, abuf, atbuf, gsnd, rdsnd, dwv, slots, qh, kh, vh, gh, rdh,
-    sbuf, dka, dva, dq, dk, dv, pbuf, csnd, cbuf,
-    g_rs, wx_rs, wz_rs, a_rs, h_rs, ga_rs, rd_rs, r_rs, b_rs, p_rs, c_rs,
-    g_ss, wx_ss, wz_ss, a_ss, h_ss, ga_ss, rd_ss, r_ss, b_ss, p_ss, c_ss,
-    loc, ga_loc, rd_loc, b_loc,
+    gbuf, wbuf, gacc, abuf, atbuf, gsnd, rdsnd, dwv, slots, qh, kh, vh, gh, rdh,
+    sbuf, dka, dva, dq, dk, dv, tbuf,
+    g_rs, wx_rs, wz_rs, a_rs, h_rs, ga_rs, rd_rs, r_rs, b_rs, t_rs,
+    g_ss, wx_ss, wz_ss, a_ss, h_ss, ga_ss, rd_ss, r_ss, b_ss, t_ss,
+    loc, ga_loc, rd_loc, b_loc, t_loc,
 ):
     dp, c, s, p, q, block = place()
     z = dp // 2
@@ -139,6 +151,8 @@
                 )
     for d in (up, down, mate):
         pl.semaphore_signal(bar, 1, device_id=(d, s), device_id_type=MESH)
+    for a in range(1, 4):
+        pl.semaphore_signal(bar, 1, device_id=(mate, block(p, (q + a) % 4)), device_id_type=MESH)
 
     lg = pltpu.make_async_copy(g_in, gbuf.at[rows(q)], loc.at[0])
     lw = pltpu.make_async_copy(w_in, wbuf.at[rows(p)], loc.at[1])
@@ -175,10 +189,10 @@
         return [(g_in.at[pl.ds(half * 64, 64)], ref)]
 
     def w_pieces(who, half):
-        refs = [wbuf.at[rows(((p + a) % 4) * 8 + who * 2 + half, 16)] for a in range(1, 4)]
+        refs = [wbuf.at[rows(((p + a) % 4) * 2 + half, 64), rows(who, 1024)] for a in range(1, 4)]
         return [(ref, ref) for ref in refs]
 
-    g_half, w_half = gbuf.at[pl.ds(0, 64)], wbuf.at[pl.ds(0, 48)]
+    g_half, w_half = gbuf.at[pl.ds(0, 64)], wbuf.at[pl.ds(0, 192), pl.ds(0, 1024)]
 
     def send_heads(t):
         src, dst = heads[t]
@@ -188,33 +202,37 @@
                     d = block((p + a) % 4, (q + b) % 4)
                     remote(src.at[:, rows(d)], dst.at[rows(s)], h_ss.at[t], h_rs.at[t], dp, d)
 
-    def ring_send():
+    def ring_put(way, step, lane, src):
+        remote(src, slots.at[way, step, lane], r_ss, r_rs.at[way, step, lane], (up, down)[way], s)
+
+    def ring_begin():
+        for lane in range(2):
+            ring_put(0, 0, lane, dwv.at[4, lane])
+            ring_put(1, 0, lane + 2, dwv.at[4, lane + 2])
+        for lane in range(2):
+            ring_put(0, 1, lane + 2, dwv.at[3, lane + 2])
+            ring_put(1, 1, lane, dwv.at[5, lane])
+
+    def ring_step(step, lanes):
+        for way, lane in enumerate(lanes):
+            got = slots.at[way, step, lane]
+            drain(got, r_rs.at[way, step, lane])
+            ahead = (3 - step, 5 + step)[way]
+            slots[way, step, lane] = (got[...].astype(F32) + dwv[ahead, lane].astype(F32)).astype(BF16)
+            ring_put(way, step + 1, lane, got)
+
+    def project(rel):
+        part = lax.dot_general(
+            atbuf[...], gbuf[:, rows((z + rel) % 8, 512)], NN, preferred_element_type=F32
+        ).astype(BF16)
         for lane in range(4):
-            remote(dwv.at[0, lane], slots.at[0, lane], r_ss, r_rs.at[0, lane], up if lane < 2 else down, s)
-
-    def ring_step(t):
-        for lane in (0, 2, 1, 3):
-            drain(slots.at[t, lane], r_rs.at[t, lane])
-            slots[t, lane] = (slots[t, lane].astype(F32) + dwv[t + 1, lane].astype(F32)).astype(BF16)
-            if t < 6:
-                remote(
-                    slots.at[t, lane], slots.at[t + 1, lane], r_ss, r_rs.at[t + 1, lane],
-                    up if lane < 2 else down, s,
-                )
-
-    def project(n):
-        for half, chunk in ((0, (z + 7 - n) % 8), (1, (z + 1 + n) % 8)):
-            part = lax.dot_general(
-                atbuf[pl.ds(half * 256, 256), :], gbuf[:, rows(chunk, 512)], NN, preferred_element_type=F32
-            ).astype(BF16)
-            dwv[n, half * 2] = part[:128]
-            dwv[n, half * 2 + 1] = part[128:]
-
-    pl.semaphore_wait(bar, 18)
+            dwv[rel, lane] = part[lane * 128 : (lane + 1) * 128]
+
+    pl.semaphore_wait(bar, 21)
     for a in (1, 3, 2):
         pp = (p + a) % 4
         remote(
-            w_in.at[rows(zq, 32)], wbuf.at[rows(p * 4 + zq, 32)], wx_ss, wx_rs.at[p], dp, block(pp, q)
+            w_in.at[:, rows(zq, 1024)], wbuf.at[rows(p), rows(zq, 1024)], wx_ss, wx_rs.at[p], dp, block(pp, q)
         )
     spread(g_pieces, q, to_next, to_prev, g_ss, g_rs)
     for b in (1, 3, 2):
@@ -225,7 +243,7 @@
             )
     for a in (1, 3, 2):
         pp = (p + a) % 4
-        drain(wbuf.at[rows(pp * 4 + zq, 32)], wx_rs.at[pp])
+        drain(wbuf.at[rows(pp), rows(zq, 1024)], wx_rs.at[pp])
     spread(w_pieces, zq, to_up, to_down, wz_ss, wz_rs)
     pass_on(g_pieces, g_half, q, to_next, to_prev, g_ss, g_rs)
     send_heads(0)
@@ -238,18 +256,26 @@
     arrive(g_half, g_rs)
     send_heads(1)
     send_heads(2)
-    pl.loop(0, 8)(project)
+    pl.loop(3, 6)(project)
     lw.wait()
-    arrive(w_half, wz_rs)
-    ring_send()
+
+    def grad_attn(quarter, begin=False):
+        cols = rows(quarter, 1024)
+        part = lax.dot_general(gbuf[:, cols], wbuf[:, cols], NT, preferred_element_type=F32)
+        gacc[...] = part if begin else gacc[...] + part
+
+    grad_attn(zq, True)
+    arrive(w_half, wz_rs, (2, 3))
+    grad_attn((zq + 3) % 4)
+    grad_attn((zq + 1) % 4)
+    arrive(w_half, wz_rs, (4, 5))
+    ring_begin()
+    grad_attn((zq + 2) % 4)
 
     for n in range(2):
-        ga = lax.dot_general(
-            gbuf[...], wbuf[pl.ds(n * 256, 256), :], NT, preferred_element_type=F32
-        ).astype(BF16)
         for m in range(2):
             f = n * 2 + m
-            gf = ga[:, m * 128 : (m + 1) * 128]
+            gf = gacc[:, f * 128 : (f + 1) * 128].astype(BF16)
             gsnd[f] = gf
             prod = gf.astype(F32) * abuf[:, f * 128 : (f + 1) * 128].astype(F32)
             rd = jnp.sum(prod.T, axis=0, keepdims=True)
@@ -270,7 +296,12 @@
                     )
                     remote(rdsnd.at[f, b], rdh.at[block(p, b)], rd_ss, rd_rs, dp, block(f, q))
 
-    ring_step(0)
+    pl.loop(6, 8)(project)
+    pl.loop(0, 3)(project)
+    todo = [(0, (0, 2)), (0, (1, 3))]
+    todo += [(step, lanes) for step in (1, 2) for lanes in ((2, 0), (3, 1), (0, 2), (1, 3))]
+    for _ in range(FIRST_STEPS):
+        ring_step(*todo.pop(0))
     dka[...] = jnp.zeros_like(dka)
     dva[...] = jnp.zeros_like(dva)
     for cp in lh:
@@ -281,11 +312,15 @@
         drain(dst.at[pl.ds(0, 1920)], h_rs.at[t])
     drain(gsnd.at[pl.ds(0, 3)], ga_rs)
     drain(rdsnd.at[pl.ds(0, 3)], rd_rs)
-    ring_step(1)
+
+
+    def go_on():
+        if len(todo) > LAST_STEPS:
+            ring_step(*todo.pop(0))
 
     back = ((dq, oq), (dk, ok), (dv, ov))
     for i in range(NBLK - 1, -1, -1):
-        attend(i, first, qh, kh, vh, gh, rdh, dq, sbuf, dka, dva)
+        attend(i, first, qh, kh, vh, gh, rdh, dq, sbuf, dka, dva, go_on if i >= 2 else lambda: None)
         qs = pl.ds(i * BLK, BLK)
         dk[qs, :] = (dka[qs, :] * SCALE).astype(BF16)
         dv[qs, :] = dva[qs, :].astype(BF16)
@@ -301,26 +336,35 @@
             def _():
                 for n, (src, dst) in enumerate(back):
                     remote(src.at[rows(d)], dst.at[:, rows(s)], b_ss.at[n], b_rs.at[n], dp, d)
-        if i in (3, 2, 0):
-            ring_step({3: 2, 2: 3, 0: 4}[i])
-    ring_step(5)
-    ring_step(6)
-
-    lp = pltpu.make_async_copy(slots.at[6, p], pbuf.at[p], loc.at[9])
-    lp.start()
-    for a in (1, 3, 2):
-        pp = (p + a) % 4
-        remote(slots.at[6, pp], pbuf.at[p], p_ss, p_rs, dp, block(pp, q))
-    lp.wait()
-    drain(pbuf.at[pl.ds(0, 3)], p_rs)
-    tot = pbuf[0].astype(F32)
-    for a in range(1, 4):
-        tot += pbuf[a].astype(F32)
-    csnd[0] = tot[:, :256]
-    csnd[1] = tot[:, 256:]
-    remote(csnd.at[1 - c], cbuf, c_ss, c_rs, mate, s)
-    drain(cbuf, c_rs)
-    ow[...] = csnd[c] + cbuf[...]
+        go_on()
+    for step in todo:
+        ring_step(*step)
+
+    drain(dwv.at[pl.ds(0, 7)], r_ss)
+    for lane in (2, 0, 3, 1):
+        drain(slots.at[0, 3, lane], r_rs.at[0, 3, lane])
+        drain(slots.at[1, 3, lane], r_rs.at[1, 3, lane])
+        dwv[4, lane] = (
+            dwv[0, lane].astype(F32) + slots[0, 3, lane].astype(F32) + slots[1, 3, lane].astype(F32)
+        ).astype(BF16)
+        for cc in range(2):
+            piece = dwv.at[4, lane, :, pl.ds(cc * 256, 256)]
+            own = (lane == p) & (cc == c)
+
+            @pl.when(own)
+            def _():
+                pltpu.make_async_copy(piece, tbuf.at[c * 4 + p], t_loc).start()
+
+            @pl.when(jnp.logical_not(own))
+            def _():
+                remote(piece, tbuf.at[c * 4 + p], t_ss, t_rs, z * 2 + cc, block(lane, q))
+
+    drain(tbuf.at[0], t_loc)
+    drain(tbuf.at[pl.ds(0, 7)], t_rs)
+    tot = tbuf[0].astype(F32)
+    for n in range(1, 8):
+        tot += tbuf[n].astype(F32)
+    ow[...] = tot
 
     for n, (src, dst) in enumerate(back):
         drain(src.at[pl.ds(0, 128)], b_loc.at[n])
@@ -332,9 +376,7 @@
     drain(abuf.at[pl.ds(0, 384)], a_ss)
     drain(gsnd.at[pl.ds(0, 3)], ga_ss)
     drain(rdsnd.at[pl.ds(0, 3)], rd_ss)
-    drain(slots, r_ss)
-    drain(pbuf.at[pl.ds(0, 3)], p_ss)
-    drain(cbuf, c_ss)
+    drain(tbuf.at[pl.ds(0, 7)], t_ss)
     for t, (src, dst) in enumerate(heads):
         drain(dst.at[pl.ds(0, 1920)], h_ss.at[t])
 
@@ -351,15 +393,16 @@
         in_specs=[any_] * 6 + [pl.BlockSpec(memory_space=pltpu.SMEM)],
         out_specs=(any_, any_, any_, pl.BlockSpec(memory_space=pltpu.VMEM)),
         scratch_shapes=[
-            pltpu.VMEM((512, 4096), BF16), pltpu.VMEM((512, 4096), BF16), pltpu.VMEM((512, 512), BF16),
+            pltpu.VMEM((512, 4096), BF16), pltpu.VMEM((512, 4096), BF16), pltpu.VMEM((512, 512), F32),
+            pltpu.VMEM((512, 512), BF16),
             pltpu.VMEM((512, 512), BF16), pltpu.VMEM((4, 512, 128), BF16), pltpu.VMEM((4, 4, 8, 128), F32),
-            pltpu.VMEM((8, 4, 128, 512), BF16), pltpu.VMEM((7, 4, 128, 512), BF16),
+            pltpu.VMEM((8, 4, 128, 512), BF16), pltpu.VMEM((2, 4, 4, 128, 512), BF16),
             head, head, head, head, pltpu.VMEM((16, 8, 128), F32),
             pltpu.VMEM((2048, BLK), F32), acc, acc, head, head, head,
-            pltpu.VMEM((4, 128, 512), BF16), pltpu.VMEM((2, 128, 256), F32), pltpu.VMEM((128, 256), F32),
-            dma((6,)), dma((4,)), dma((6,)), dma, dma((3,)), dma, dma, dma((7, 4)), dma((3,)), dma, dma,
-            dma, dma, dma, dma, dma((3,)), dma, dma, dma, dma((3,)), dma, dma,
-            dma((10,)), dma, dma, dma((3,)),
+            pltpu.VMEM((8, 128, 256), BF16),
+            dma((6,)), dma((4,)), dma((6,)), dma, dma((3,)), dma, dma, dma((2, 4, 4)), dma((3,)), dma,
+            dma, dma, dma, dma, dma((3,)), dma, dma, dma, dma((3,)), dma,
+            dma((9,)), dma, dma, dma((3,)), dma,
         ],
         compiler_params=pltpu.CompilerParams(collective_id=0, has_side_effects=True, vmem_limit_bytes=VMEM_LIMIT),
         name="whole",

time: 107 us -> 101 us (0.944)
  Pallas kernels: 106 us -> 100 us
    pallas_call x1, Pallas kernels: 104 us -> 97.4 us  [run_whole(): pl.pallas_call(whole_kernel, out_shape=(tok, tok, tok, jax.ShapeDtypeStru...]
where the time goes in v4:
time: 101 us
  Pallas kernels  100 us (99%)
    pallas_call x1, Pallas kernels, run_whole(): pl.pallas_call(whole_kernel, out_shape=(tok, tok, tok, jax.ShapeDtypeStru...  97.4 us
    pallas_call x1, Pallas kernels, finish(): pl.pallas_call(finish_kernel, out_shape=tuple((jax.ShapeDtypeStruct(a.sha...  2.59 us

profile of v4, /device:TPU:1, one launch (start us, length us, event | category | flops | bytes accessed | tf_op | source)
XLA Modules:
  0.0 100.7 jit_solution(2156719101808034905)
XLA Ops:
  0.6 97.4 %whole.1 = (bf16[128,2048]{1,0:T(8,128)(2,1)}, bf16[128,2048]{1,0:T(8,128)(2,1)}, bf16[128,2048]{1,0:T(8,128)(2,1)}, f32[128,256]{1,0:T(8,128)}) custom-call(bf16[128,2048]{1,0:T(8,128)(2,1)} %q_in.1, bf16[128,2048]{1,0:T(8,128)(2,1)} %k_in.1, bf16[128,2048]{1,0:T(8,128)(2,1)} %v_in.1, bf16[128,2048]{1,0:T(8,128)(2,1)} %o_in.1, bf16[128,4096]{1,0:T(8,128)(2,1)} %g_in.1, ...), custom_call_target="tpu_custom_call" | custom-call | tf_op jit(solution)/shard_map/whole/pallas_call | solution.py:390
  98.1 2.6 %finish.1 = (bf16[128,2048]{1,0:T(8,128)(2,1)}, bf16[128,2048]{1,0:T(8,128)(2,1)}, bf16[128,2048]{1,0:T(8,128)(2,1)}, f32[128,256]{1,0:T(8,128)}) custom-call(bf16[128,2048]{1,0:T(8,128)(2,1)} %get-tuple-element.8.refs_0_, bf16[128,2048]{1,0:T(8,128)(2,1)} %get-tuple-element.9.refs_1_, bf16[128,2048]{1,0:T(8,128)(2,1)} %get-tuple-element.10.refs_2_, ...), custom_call_target="tpu_custom_call" | custom-call | tf_op jit(solution)/shard_map/finish/pallas_call | solution.py:420

commit v5 on v4

--- a/solution.py
+++ b/solution.py
@@ -51,7 +51,7 @@
 NBLK = 2048 // BLK
 SCALE = HDIM ** (-0.5)
 LOG2E = 1.4426950408889634
-FIRST_STEPS = 3
+FIRST_STEPS = 1
 LAST_STEPS = 2
 
 
@@ -61,13 +61,13 @@
             send(src, dst, ss, rs.at[sem])
 
 
-def pass_on(pieces, whole, me, send_next, send_prev, ss, rs):
+def pass_on(pieces, relayed, whole, me, send_next, send_prev, ss, rs):
     nxt, prv = (me + 1) % 4, (me + 3) % 4
     drain(whole, rs.at[0])
-    for _, ref in pieces(prv, 0):
+    for _, ref in relayed(prv, 0):
         send_next(ref, ref, ss, rs.at[4])
     drain(whole, rs.at[1])
-    for _, ref in pieces(nxt, 1):
+    for _, ref in relayed(nxt, 1):
         send_prev(ref, ref, ss, rs.at[5])
 
 
@@ -76,55 +76,50 @@
         drain(whole, rs.at[sem])
 
 
-def attend(i, first, q, k, v, g, rd, dq, sbuf, dka, dva, between):
+def pair(i, j):
+    return pl.ds((i * (i + 1) // 2 + j) * BLK, BLK)
+
+
+def weigh(i, first, q, k, sbuf):
     qs = pl.ds(i * BLK, BLK)
     pos = lax.broadcasted_iota(jnp.int32, (1, BLK), 1) + i * BLK
     seg = jnp.zeros((1, BLK), jnp.int32)
     for e in range(8):
         st = first[0, e]
         seg = jnp.where(pos >= st, jnp.maximum(seg, st), seg)
-    rdi = jnp.concatenate([rd[i * (BLK // 128) + t][:1] for t in range(BLK // 128)], axis=1)
-
-    def scores(j, m):
-        ks = pl.ds(j * BLK, BLK)
-        sc = lax.dot_general(k[ks, :], q[qs, :], NT, preferred_element_type=F32) * (SCALE * LOG2E)
-        kp = lax.broadcasted_iota(jnp.int32, (BLK, BLK), 0)
+    kp = lax.broadcasted_iota(jnp.int32, (BLK, BLK), 0)
+    m = jnp.full((8, BLK), -1e30, F32)
+    for j in range(i + 1):
+        sc = lax.dot_general(
+            k[pl.ds(j * BLK, BLK), :], q[qs, :], NT, preferred_element_type=F32
+        ) * (SCALE * LOG2E)
         live = kp >= seg - j * BLK
         if j == i:
             live = live & (kp <= pos - j * BLK)
         sc = jnp.where(live, sc, -1e30)
-        sbuf[ks, :] = sc
-        return jnp.maximum(m, jnp.max(sc.reshape(BLK // 8, 8, BLK), axis=0))
-
-    m = jnp.full((8, BLK), -1e30, F32)
-    for j in range(i + 1):
-        m = scores(j, m)
+        sbuf[pair(i, j), :] = sc
+        m = jnp.maximum(m, jnp.max(sc.reshape(BLK // 8, 8, BLK), axis=0))
     m = jnp.max(m, axis=0, keepdims=True)
-
-    def expo(j, tot):
-        ks = pl.ds(j * BLK, BLK)
-        e = jnp.exp2(sbuf[ks, :] - m)
-        sbuf[ks, :] = e
-        return tot + jnp.sum(e.reshape(BLK // 8, 8, BLK), axis=0)
-
     tot = jnp.zeros((8, BLK), F32)
     for j in range(i + 1):
-        tot = expo(j, tot)
-    inv = 1.0 / jnp.sum(tot, axis=0, keepdims=True)
-    between()
-
-    def grads(j, acc):
+        e = jnp.exp2(sbuf[pair(i, j), :] - m)
+        sbuf[pair(i, j), :] = e
+        tot = tot + jnp.sum(e.reshape(BLK // 8, 8, BLK), axis=0)
+    return 1.0 / jnp.sum(tot, axis=0, keepdims=True)
+
+
+def attend(i, inv, q, k, v, g, rd, dq, sbuf, dka, dva):
+    qs = pl.ds(i * BLK, BLK)
+    rdi = jnp.concatenate([rd[i * (BLK // 128) + t][:1] for t in range(BLK // 128)], axis=1)
+    acc = jnp.zeros((BLK, HDIM), F32)
+    for j in range(i + 1):
         ks = pl.ds(j * BLK, BLK)
-        prob = sbuf[ks, :] * inv
+        prob = sbuf[pair(i, j), :] * inv
         gp = lax.dot_general(v[ks, :], g[qs, :], NT, preferred_element_type=F32)
         ds = (prob * (gp - rdi)).astype(BF16)
         dva[ks, :] += lax.dot_general(prob.astype(BF16), g[qs, :], NN, preferred_element_type=F32)
         dka[ks, :] += lax.dot_general(ds, q[qs, :], NN, preferred_element_type=F32)
-        return acc + lax.dot_general(ds, k[ks, :], TN, preferred_element_type=F32)
-
-    acc = jnp.zeros((BLK, HDIM), F32)
-    for j in range(i + 1):
-        acc = grads(j, acc)
+        acc = acc + lax.dot_general(ds, k[ks, :], TN, preferred_element_type=F32)
     dq[qs, :] = (acc * SCALE).astype(BF16)
 
 
@@ -133,7 +128,7 @@
     oq, ok, ov, ow,
     gbuf, wbuf, gacc, abuf, atbuf, gsnd, rdsnd, dwv, slots, qh, kh, vh, gh, rdh,
     sbuf, dka, dva, dq, dk, dv, tbuf,
-    g_rs, wx_rs, wz_rs, a_rs, h_rs, ga_rs, rd_rs, r_rs, b_rs, t_rs,
+    g_rs, wx_rs, wy_rs, wz_rs, a_rs, h_rs, ga_rs, rd_rs, r_rs, b_rs, t_rs,
     g_ss, wx_ss, wz_ss, a_ss, h_ss, ga_ss, rd_ss, r_ss, b_ss, t_ss,
     loc, ga_loc, rd_loc, b_loc, t_loc,
 ):
@@ -192,6 +187,10 @@
         refs = [wbuf.at[rows(((p + a) % 4) * 2 + half, 64), rows(who, 1024)] for a in range(1, 4)]
         return [(ref, ref) for ref in refs]
 
+    def w_relayed(who, half):
+        refs = [wbuf.at[rows(((p + a) % 4) * 2 + half, 64), rows(who * 2 + 1, 512)] for a in range(1, 4)]
+        return [(ref, ref) for ref in refs]
+
     g_half, w_half = gbuf.at[pl.ds(0, 64)], wbuf.at[pl.ds(0, 192), pl.ds(0, 1024)]
 
     def send_heads(t):
@@ -235,6 +234,12 @@
             w_in.at[:, rows(zq, 1024)], wbuf.at[rows(p), rows(zq, 1024)], wx_ss, wx_rs.at[p], dp, block(pp, q)
         )
     spread(g_pieces, q, to_next, to_prev, g_ss, g_rs)
+    far = (zq + 2) % 4 * 2
+    for a in (1, 3, 2):
+        pp = (p + a) % 4
+        remote(
+            w_in.at[:, rows(far, 512)], wbuf.at[rows(p), rows(far, 512)], wx_ss, wy_rs.at[p], dp, block(pp, q)
+        )
     for b in (1, 3, 2):
         qq = (q + b) % 4
         for f in range(4):
@@ -245,13 +250,13 @@
         pp = (p + a) % 4
         drain(wbuf.at[rows(pp), rows(zq, 1024)], wx_rs.at[pp])
     spread(w_pieces, zq, to_up, to_down, wz_ss, wz_rs)
-    pass_on(g_pieces, g_half, q, to_next, to_prev, g_ss, g_rs)
+    pass_on(g_pieces, g_pieces, g_half, q, to_next, to_prev, g_ss, g_rs)
     send_heads(0)
     for cp in la:
         cp.wait()
     drain(abuf.at[pl.ds(0, 384)], a_rs)
     atbuf[...] = abuf[...].T
-    pass_on(w_pieces, w_half, zq, to_up, to_down, wz_ss, wz_rs)
+    pass_on(w_pieces, w_relayed, w_half, zq, to_up, to_down, wz_ss, wz_rs)
     lg.wait()
     arrive(g_half, g_rs)
     send_heads(1)
@@ -268,7 +273,10 @@
     arrive(w_half, wz_rs, (2, 3))
     grad_attn((zq + 3) % 4)
     grad_attn((zq + 1) % 4)
-    arrive(w_half, wz_rs, (4, 5))
+    arrive(wbuf.at[pl.ds(0, 192), pl.ds(0, 512)], wz_rs, (4, 5))
+    for a in (1, 3, 2):
+        pp = (p + a) % 4
+        drain(wbuf.at[rows(pp), rows(far, 512)], wy_rs.at[pp])
     ring_begin()
     grad_attn((zq + 2) % 4)
 
@@ -306,21 +314,27 @@
     dva[...] = jnp.zeros_like(dva)
     for cp in lh:
         cp.wait()
-    drain(gsnd.at[0], ga_loc)
-    drain(rdsnd.at[0], rd_loc)
-    for t, (src, dst) in enumerate(heads):
-        drain(dst.at[pl.ds(0, 1920)], h_rs.at[t])
-    drain(gsnd.at[pl.ds(0, 3)], ga_rs)
-    drain(rdsnd.at[pl.ds(0, 3)], rd_rs)
-
 
     def go_on():
         if len(todo) > LAST_STEPS:
             ring_step(*todo.pop(0))
 
+    drain(qh.at[pl.ds(0, 1920)], h_rs.at[0])
+    drain(kh.at[pl.ds(0, 1920)], h_rs.at[1])
+    inv = [None] * NBLK
+    for i in range(NBLK - 1, -1, -1):
+        inv[i] = weigh(i, first, qh, kh, sbuf)
+        if i >= 2:
+            go_on()
+    drain(vh.at[pl.ds(0, 1920)], h_rs.at[2])
+    drain(gsnd.at[0], ga_loc)
+    drain(rdsnd.at[0], rd_loc)
+    drain(gsnd.at[pl.ds(0, 3)], ga_rs)
+    drain(rdsnd.at[pl.ds(0, 3)], rd_rs)
+
     back = ((dq, oq), (dk, ok), (dv, ov))
     for i in range(NBLK - 1, -1, -1):
-        attend(i, first, qh, kh, vh, gh, rdh, dq, sbuf, dka, dva, go_on if i >= 2 else lambda: None)
+        attend(i, inv[i], qh, kh, vh, gh, rdh, dq, sbuf, dka, dva)
         qs = pl.ds(i * BLK, BLK)
         dk[qs, :] = (dka[qs, :] * SCALE).astype(BF16)
         dv[qs, :] = dva[qs, :].astype(BF16)
@@ -371,8 +385,8 @@
         drain(src.at[pl.ds(0, 1920)], b_rs.at[n])
         drain(src.at[pl.ds(0, 1920)], b_ss.at[n])
     drain(gbuf.at[pl.ds(0, 384)], g_ss)
-    drain(wbuf.at[pl.ds(0, 96)], wx_ss)
-    drain(wbuf.at[pl.ds(0, 288)], wz_ss)
+    drain(wbuf.at[pl.ds(0, 144)], wx_ss)
+    drain(wbuf.at[pl.ds(0, 240)], wz_ss)
     drain(abuf.at[pl.ds(0, 384)], a_ss)
     drain(gsnd.at[pl.ds(0, 3)], ga_ss)
     drain(rdsnd.at[pl.ds(0, 3)], rd_ss)
@@ -398,9 +412,9 @@
             pltpu.VMEM((512, 512), BF16), pltpu.VMEM((4, 512, 128), BF16), pltpu.VMEM((4, 4, 8, 128), F32),
             pltpu.VMEM((8, 4, 128, 512), BF16), pltpu.VMEM((2, 4, 4, 128, 512), BF16),
             head, head, head, head, pltpu.VMEM((16, 8, 128), F32),
-            pltpu.VMEM((2048, BLK), F32), acc, acc, head, head, head,
+            pltpu.VMEM((NBLK * (NBLK + 1) // 2 * BLK, BLK), F32), acc, acc, head, head, head,
             pltpu.VMEM((8, 128, 256), BF16),
-            dma((6,)), dma((4,)), dma((6,)), dma, dma((3,)), dma, dma, dma((2, 4, 4)), dma((3,)), dma,
+            dma((6,)), dma((4,)), dma((4,)), dma((6,)), dma, dma((3,)), dma, dma, dma((2, 4, 4)), dma((3,)), dma,
             dma, dma, dma, dma, dma((3,)), dma, dma, dma, dma((3,)), dma,
             dma((9,)), dma, dma, dma((3,)), dma,
         ],

time: 101 us -> 98.9 us (0.979)
  Pallas kernels: 100 us -> 97.9 us
    pallas_call x1, Pallas kernels: 97.4 us -> 95.3 us  [run_whole(): pl.pallas_call(whole_kernel, out_shape=(tok, tok, tok, jax.ShapeDtypeStru...]
where the time goes in v5:
time: 98.9 us; the launch traced here: 98.5 us
  Pallas kernels  97.9 us (99%)
    pallas_call x1, Pallas kernels, run_whole(): pl.pallas_call(whole_kernel, out_shape=(tok, tok, tok, jax.ShapeDtypeStru...  95.3 us
    pallas_call x1, Pallas kernels, finish(): pl.pallas_call(finish_kernel, out_shape=tuple((jax.ShapeDtypeStruct(a.sha...  2.59 us

profile of v5, /device:TPU:1, one launch (start us, length us, event | category | flops | bytes accessed | tf_op | source)
XLA Modules:
  0.0 98.5 jit_solution(9388941773500083942)
XLA Ops:
  0.6 95.3 %whole.1 = (bf16[128,2048]{1,0:T(8,128)(2,1)}, bf16[128,2048]{1,0:T(8,128)(2,1)}, bf16[128,2048]{1,0:T(8,128)(2,1)}, f32[128,256]{1,0:T(8,128)}) custom-call(bf16[128,2048]{1,0:T(8,128)(2,1)} %q_in.1, bf16[128,2048]{1,0:T(8,128)(2,1)} %k_in.1, bf16[128,2048]{1,0:T(8,128)(2,1)} %v_in.1, bf16[128,2048]{1,0:T(8,128)(2,1)} %o_in.1, bf16[128,4096]{1,0:T(8,128)(2,1)} %g_in.1, ...), custom_call_target="tpu_custom_call" | custom-call | tf_op jit(solution)/shard_map/whole/pallas_call | solution.py:404
  95.9 2.6 %finish.1 = (bf16[128,2048]{1,0:T(8,128)(2,1)}, bf16[128,2048]{1,0:T(8,128)(2,1)}, bf16[128,2048]{1,0:T(8,128)(2,1)}, f32[128,256]{1,0:T(8,128)}) custom-call(bf16[128,2048]{1,0:T(8,128)(2,1)} %get-tuple-element.8.refs_0_, bf16[128,2048]{1,0:T(8,128)(2,1)} %get-tuple-element.9.refs_1_, bf16[128,2048]{1,0:T(8,128)(2,1)} %get-tuple-element.10.refs_2_, ...), custom_call_target="tpu_custom_call" | custom-call | tf_op jit(solution)/shard_map/finish/pallas_call | solution.py:434
